TPU v7x, 32 devices: a whole 2x2x4 slice. The times are simulated.
32 devices in a mesh: dp: 8 (over z, y), tensor: 4 (over x, core).
Axes of the slice: x: 2, y: 2, z: 4, core: 2. Of those that a mesh axis runs over, the one named last changes fastest.
Arguments:
- hidden_in: bfloat16 [32, 1024, 480], P('dp', 'tensor'), may hold values from -6 to 6
- attn_gain: float32 [480], replicated, may hold values from 0.25 to 1.75
- attn_shift: float32 [480], replicated, may hold values from -1.75 to 1.75
- query_key_value_weight: bfloat16 [3, 480, 480], P(None, None, 'tensor'), may hold values from -0.25 to 0.25
- query_key_value_bias: float32 [3, 480], P(None, 'tensor'), may hold values from -1.75 to 1.75
- attention_output_weight: bfloat16 [480, 480], P('tensor'), may hold values from -3.5 to 3.5
- out_bias: float32 [480], replicated, may hold values from -1.75 to 1.75
- ffn_gain: float32 [480], replicated, may hold values from 0.25 to 1.75
- ffn_shift: float32 [480], replicated, may hold values from -1.75 to 1.75
- up_projection_weight: bfloat16 [480, 1920], P('tensor', 'dp'), may hold values from -0.25 to 0.25
- up_projection_bias: float32 [1920], replicated, may hold values from -3 to 3
- down_projection_weight: bfloat16 [1920, 480], P('dp', 'tensor'), may hold values from -0.125 to 0.125
- down_bias: float32 [480], replicated, may hold values from -1.75 to 1.75
- lengths: int32 [32], P('dp'), may hold values from 204 to 1024, as said below
- cotangent: bfloat16 [32, 1024, 480], P('dp', 'tensor'), may hold values from -6 to 6
Outputs:
- hidden_out: bfloat16 [32, 1024, 480], P('dp', 'tensor')
- grad_hidden: bfloat16 [32, 1024, 480], P('dp', 'tensor')
- grad_attn_gain: float32 [480], replicated
- grad_attn_shift: float32 [480], replicated
- grad_qkv_weight: float32 [3, 480, 480], P(None, None, 'tensor')
- grad_qkv_bias: float32 [3, 480], P(None, 'tensor')
- grad_out_weight: float32 [480, 480], P('tensor')
- grad_out_bias: float32 [480], replicated
- grad_ffn_gain: float32 [480], replicated
- grad_ffn_shift: float32 [480], replicated
- grad_up_weight: float32 [480, 1920], P('tensor', 'dp')
- grad_up_bias: float32 [1920], replicated
- grad_down_weight: float32 [1920, 480], P('dp', 'tensor')
- grad_down_bias: float32 [480], replicated
Inputs may be any that keep to these rules, and one draw needn't show every extreme that they name: `lengths`: every index of dp holds at least one row longer than 768, and some row has exactly 1024.
All inputs are finite; a program needn't handle non-finite values.
Results may differ from a plain program's by a relative error of at most 0.012.
Values may be sent and summed in bfloat16 or wider, within the bound.
No kernel may reach another device: no remote copies, remote signals or barrier semaphores. Data moves between devices by JAX's collectives and lax.ppermute only.
A program may use at most 192 MiB of HBM per device.

v0:
```python
from functools import partial

import jax
import jax.numpy as jnp
from jax import lax
from jax.sharding import PartitionSpec as P

HEAD_DIM = 24


EPS = 1e-05
MASK_FILL = -1000000000.0


def norm_parts(values, norm_gain, norm_shift):
    centre = values - jnp.mean(values, axis=-1, keepdims=True)
    inverse = lax.rsqrt(jnp.mean(centre * centre, axis=-1, keepdims=True) + EPS)
    unit_rows = centre * inverse
    return (unit_rows * norm_gain + norm_shift, unit_rows, inverse)


def norm_back(upstream, unit_rows, inverse, norm_gain):
    scaled = upstream * norm_gain
    centred = scaled - jnp.mean(scaled, axis=-1, keepdims=True)
    return inverse * (centred - unit_rows * jnp.mean(scaled * unit_rows, axis=-1, keepdims=True))


def rotary_tables(length, head_dim):
    frequency = 1.0 / 10000.0 ** (jnp.arange(0, head_dim, 2).astype(jnp.float32) / head_dim)
    angles = jnp.arange(length).astype(jnp.float32)[:, None] * frequency[None, :]
    angles = jnp.concatenate([angles, angles], axis=-1)
    return (jnp.cos(angles), jnp.sin(angles))


def rotate(values, cosine_table, sine_table):
    half_dim = values.shape[-1] // 2
    turned = jnp.concatenate([-values[..., half_dim:], values[..., :half_dim]], axis=-1)
    return values * cosine_table + turned * sine_table


def rotate_back(values, cosine_table, sine_table):
    half_dim = values.shape[-1] // 2
    moved = values * sine_table
    return values * cosine_table + jnp.concatenate(
        [moved[..., half_dim:], -moved[..., :half_dim]], axis=-1
    )


def shards(
    hidden_in,
    attn_gain,
    attn_shift,
    query_key_value_weight,
    query_key_value_bias,
    attention_output_weight,
    out_bias,
    ffn_gain,
    ffn_shift,
    up_projection_weight,
    up_projection_bias,
    down_projection_weight,
    down_bias,
    lengths,
    cotangent,
):
    tensor_count = lax.axis_size("tensor")
    seq_count, local_len, model_width = hidden_in.shape
    full_len = local_len * tensor_count
    local_heads = query_key_value_weight.shape[2] // HEAD_DIM
    query_scale = HEAD_DIM ** (-0.5)
    positions = jnp.arange(full_len)
    cosine_table, sine_table = rotary_tables(full_len, HEAD_DIM)
    inputs = hidden_in.astype(jnp.float32)
    first_normalized, unit_one, inverse_one = norm_parts(inputs, attn_gain, attn_shift)
    collected_rows, up_part, down_part = (
        lax.all_gather(first_normalized.astype(jnp.bfloat16), "tensor", axis=1, tiled=True),
        lax.all_gather(up_projection_weight, "tensor", axis=0, tiled=True),
        lax.all_gather(down_projection_weight, "tensor", axis=1, tiled=True),
    )
    attention_projected = jnp.einsum(
        "ugb,tba->tuga", collected_rows, query_key_value_weight, preferred_element_type=jnp.float32
    )
    attention_projected = attention_projected + query_key_value_bias[:, None, None, :]
    split_heads = attention_projected.reshape(
        3, seq_count, full_len, local_heads, HEAD_DIM
    ).transpose(0, 1, 3, 2, 4)
    queries = rotate(split_heads[0] * query_scale, cosine_table, sine_table).astype(jnp.bfloat16)
    key_rows = rotate(split_heads[1], cosine_table, sine_table).astype(jnp.bfloat16)
    value_rows = split_heads[2].astype(jnp.bfloat16)

    def masked_scores(query_one, key_one, row_length):
        scores = jnp.einsum("hqd,hkd->hqk", query_one, key_one, preferred_element_type=jnp.float32)
        return jnp.where((positions < row_length)[None, None, :], scores, MASK_FILL)

    def attend(pieces):
        query_one, key_one, value_one, row_length = pieces
        scores = masked_scores(query_one, key_one, row_length)
        row_peak = jnp.max(scores, axis=-1, keepdims=True)
        exponent = jnp.exp(scores - row_peak)
        row_total = jnp.sum(exponent, axis=-1, keepdims=True)
        prob_low = (exponent / row_total).astype(jnp.bfloat16)
        mixed_one = jnp.einsum(
            "hqk,hkd->hqd", prob_low, value_one, preferred_element_type=jnp.float32
        )
        return (mixed_one, row_peak[..., 0] + jnp.log(row_total[..., 0]))

    blended_rows, logsum = lax.map(attend, (queries, key_rows, value_rows, lengths))
    blended_narrow = (
        blended_rows.transpose(0, 2, 1, 3).reshape(seq_count, full_len, -1).astype(jnp.bfloat16)
    )
    partial_branch = jnp.einsum(
        "ovx,xc->ovc", blended_narrow, attention_output_weight, preferred_element_type=jnp.float32
    )
    residual_branch = lax.psum_scatter(partial_branch, "tensor", scatter_dimension=1, tiled=True)
    middle = inputs + residual_branch + out_bias
    second_normalized, unit_two, inverse_two = norm_parts(middle, ffn_gain, ffn_shift)
    second_normalized_narrow = second_normalized.astype(jnp.bfloat16)
    up_projection_total, down_projection_total = (
        lax.all_gather(up_part, "dp", axis=1, tiled=True),
        lax.all_gather(down_part, "dp", axis=0, tiled=True),
    )
    up_projected = (
        jnp.einsum(
            "ujr,rg->ujg",
            second_normalized_narrow,
            up_projection_total,
            preferred_element_type=jnp.float32,
        )
        + up_projection_bias
    )
    gelu_output, gelu_pull = jax.vjp(partial(jax.nn.gelu, approximate=False), up_projected)
    gelu_output_narrow = gelu_output.astype(jnp.bfloat16)
    down_projected = jnp.einsum(
        "jbz,zq->jbq", gelu_output_narrow, down_projection_total, preferred_element_type=jnp.float32
    )
    hidden_out = (middle + down_projected + down_bias).astype(jnp.bfloat16)
    upstream = cotangent.astype(jnp.float32)
    grad_down_full = jnp.einsum(
        "qkg,qkm->gm", gelu_output_narrow, cotangent, preferred_element_type=jnp.float32
    )
    grad_down_bias = jnp.sum(upstream, axis=(0, 1))
    gelu_gradient = jnp.einsum(
        "omy,iy->omi", cotangent, down_projection_total, preferred_element_type=jnp.float32
    )
    grad_up = gelu_pull(gelu_gradient)[0]
    grad_up_bias = jnp.sum(grad_up, axis=(0, 1))
    up_gradient_narrow = grad_up.astype(jnp.bfloat16)
    grad_up_full = jnp.einsum(
        "ioh,ioq->hq",
        second_normalized_narrow,
        up_gradient_narrow,
        preferred_element_type=jnp.float32,
    )
    grad_normed_two = jnp.einsum(
        "jag,bg->jab", up_gradient_narrow, up_projection_total, preferred_element_type=jnp.float32
    )
    grad_ffn_gain = jnp.sum(grad_normed_two * unit_two, axis=(0, 1))
    grad_ffn_shift = jnp.sum(grad_normed_two, axis=(0, 1))
    grad_middle = upstream + norm_back(grad_normed_two, unit_two, inverse_two, ffn_gain)
    grad_out_bias = jnp.sum(grad_middle, axis=(0, 1))
    grad_branch = grad_middle.astype(jnp.bfloat16)
    gradient_rows = lax.all_gather(grad_branch, "tensor", axis=1, tiled=True)
    grad_out_local = jnp.einsum(
        "urw,ura->wa", blended_narrow, gradient_rows, preferred_element_type=jnp.float32
    )
    grad_mixed = jnp.einsum(
        "noy,iy->noi", gradient_rows, attention_output_weight, preferred_element_type=jnp.float32
    ).astype(jnp.bfloat16)
    grad_mixed = grad_mixed.reshape(seq_count, full_len, local_heads, HEAD_DIM).transpose(
        0, 2, 1, 3
    )

    def attend_back(pieces):
        query_one, key_one, value_one, row_length, logsum_one, grad_one = pieces
        scores = masked_scores(query_one, key_one, row_length)
        probs_full = jnp.exp(scores - logsum_one[..., None])
        grad_values = jnp.einsum(
            "hqk,hqd->hkd",
            probs_full.astype(jnp.bfloat16),
            grad_one,
            preferred_element_type=jnp.float32,
        )
        grad_probs = jnp.einsum(
            "hqd,hkd->hqk", grad_one, value_one, preferred_element_type=jnp.float32
        )
        inner_sum = jnp.sum(probs_full * grad_probs, axis=-1, keepdims=True)
        grad_scores = (probs_full * (grad_probs - inner_sum)).astype(jnp.bfloat16)
        grad_queries = jnp.einsum(
            "hqk,hkd->hqd", grad_scores, key_one, preferred_element_type=jnp.float32
        )
        grad_keys = jnp.einsum(
            "hqk,hqd->hkd", grad_scores, query_one, preferred_element_type=jnp.float32
        )
        return (grad_queries, grad_keys, grad_values)

    grad_queries, grad_keys, grad_values = lax.map(
        attend_back, (queries, key_rows, value_rows, lengths, logsum, grad_mixed)
    )
    grad_query_pre = rotate_back(grad_queries, cosine_table, sine_table) * query_scale
    grad_key_pre = rotate_back(grad_keys, cosine_table, sine_table)
    grad_projected = jnp.stack([grad_query_pre, grad_key_pre, grad_values])
    grad_projected = grad_projected.transpose(0, 1, 3, 2, 4).reshape(3, seq_count, full_len, -1)
    grad_bias_local = jnp.sum(grad_projected, axis=(1, 2))
    projection_gradient_narrow = grad_projected.astype(jnp.bfloat16)
    grad_qkv_local = jnp.einsum(
        "nth,xntv->xhv",
        collected_rows,
        projection_gradient_narrow,
        preferred_element_type=jnp.float32,
    )
    grad_normed_part = jnp.einsum(
        "rfmp,rip->fmi",
        projection_gradient_narrow,
        query_key_value_weight,
        preferred_element_type=jnp.float32,
    )
    grad_normed = lax.psum_scatter(grad_normed_part, "tensor", scatter_dimension=1, tiled=True)
    grad_attn_gain = jnp.sum(grad_normed * unit_one, axis=(0, 1))
    grad_attn_shift = jnp.sum(grad_normed, axis=(0, 1))
    grad_hidden = (grad_middle + norm_back(grad_normed, unit_one, inverse_one, attn_gain)).astype(
        jnp.bfloat16
    )
    grad_qkv_weight, grad_qkv_bias, grad_out_weight = lax.psum(
        (grad_qkv_local, grad_bias_local, grad_out_local), "dp"
    )
    (
        grad_attn_gain,
        grad_attn_shift,
        grad_out_bias,
        grad_ffn_gain,
        grad_ffn_shift,
        grad_up_bias,
        grad_down_bias,
    ) = lax.psum(
        (
            grad_attn_gain,
            grad_attn_shift,
            grad_out_bias,
            grad_ffn_gain,
            grad_ffn_shift,
            grad_up_bias,
            grad_down_bias,
        ),
        ("dp", "tensor"),
    )
    grad_up_part, grad_down_part = (
        lax.psum_scatter(grad_up_full, "dp", scatter_dimension=1, tiled=True),
        lax.psum_scatter(grad_down_full, "dp", scatter_dimension=0, tiled=True),
    )
    grad_up_weight, grad_down_weight = (
        lax.psum_scatter(grad_up_part, "tensor", scatter_dimension=0, tiled=True),
        lax.psum_scatter(grad_down_part, "tensor", scatter_dimension=1, tiled=True),
    )
    return (
        hidden_out,
        grad_hidden,
        grad_attn_gain,
        grad_attn_shift,
        grad_qkv_weight,
        grad_qkv_bias,
        grad_out_weight,
        grad_out_bias,
        grad_ffn_gain,
        grad_ffn_shift,
        grad_up_weight,
        grad_up_bias,
        grad_down_weight,
        grad_down_bias,
    )


def solution(mesh):
    return jax.shard_map(
        shards,
        mesh=mesh,
        in_specs=(
            P("dp", "tensor", None),
            P(),
            P(),
            P(None, None, "tensor"),
            P(None, "tensor"),
            P("tensor", None),
            P(),
            P(),
            P(),
            P("tensor", "dp"),
            P(),
            P("dp", "tensor"),
            P(),
            P("dp"),
            P("dp", "tensor", None),
        ),
        out_specs=(
            P("dp", "tensor", None),
            P("dp", "tensor", None),
            P(),
            P(),
            P(None, None, "tensor"),
            P(None, "tensor"),
            P("tensor", None),
            P(),
            P(),
            P(),
            P("tensor", "dp"),
            P(),
            P("dp", "tensor"),
            P(),
        ),
        check_vma=False,
    )
```

profile of v0, /device:TPU:0, one launch (start us, length us, event | category | flops | bytes accessed | tf_op | source)
XLA Modules:
  0.0 844.9 jit_solution(6292052115918659769)
XLA Ops:
  15.8 34.7 %all-gather.5.cloned.1.call-done = bf16[4,1024,480]{1,2,0:T(8,128)(2,1)} async-done(((bf16[4,256,480]{1,2,0:T(8,128)(2,1)}), bf16[4,1024,480]{1,2,0:T(8,128)(2,1)}) %all-gather.5.cloned.1.call-update) | async-done | bytes 3932176 | tf_op jit(solution)/shard_map/all_gather | solution.py:76
  60.1 65.2 %while.30 = (s32[]{:T(128)}, bf16[4,5,1024,24]{2,3,1,0:T(8,128)(2,1)}, f32[4,5,1024]{2,1,0:T(8,128)}, s32[4]{0:T(128)S(1)}, bf16[4,5,1024,24]{2,3,1,0:T(8,128)(2...) while((s32[]{:T(128)}, ...), condition=%wide.region_5.6_spmd.clone.clone, body=%wide.region_2.5_spmd.clone.sunk.clone | while | flops 550498304 | bytes 64325736 | solution.py:107
  145.7 54.4 %reduce-scatter.11.cloned.1.call-done = f32[4,256,480]{1,2,0:T(8,128)} async-done(((f32[4,1024,480]{1,2,0:T(8,128)}), f32[4,256,480]{1,2,0:T(8,128)}) %reduce-scatter.11.cloned.1.call-update) | async-done | bytes 1966096 | tf_op jit(solution)/shard_map/reduce_scatter | solution.py:114
  205.1 6.8 fusion.99
  215.1 19.0 %multiply_convert_fusion.1 = (bf16[4,256,1920]{2,1,0:T(8,128)(2,1)}, f32[4,256,1920]{2,1,0:T(8,128)}) fusion(f32[4,256,1920]{2,1,0:T(8,128)S(1)} %get-tuple-element.296, f32[1920]{0:T(1024)S(1)} %copy-done.33, u8[256,1920]{1,0:T(8,128)(4,1)S(1)} %get-tuple-element.216, u8[256,1920]{1,0:T(8,128)(4,1)S(1)} %get-tuple-element.215), kind=kLoop, calls=%fused_computation.65 | loop fusion | flops 139591680 | bytes 20651520 | tf_op jit(solution)/shard_map/convert_element_type | solution.py:132
  235.6 9.5 %fusion.120 = (f32[1920]{0:T(1024)}, bf16[4,256,1920]{2,1,0:T(8,128)(2,1)S(1)}) fusion(f32[4,256,1920]{2,1,0:T(8,128)} %get-tuple-element.271, bf16[4,256,480]{1,2,0:T(8,128)(2,1)S(1)} %copy-done.16, bf16[1920,480]{1,0:T(8,128)(2,1)} %all-gather.9.cloned.1.call-done, f32[4,256,1920]{2,1,0:T(8,128)} %copy-done.13, f32[1920]{0:T(1024)S(1)} %copy-done.33), kind=kOutput, calls=%fused_computation.179 | convolution fusion | flops 1918892160 | bytes 22502400 | tf_op jit(solution)/shard_map/omy,iy->omi/dot_general | solution.py:142
  245.1 6.3 multiply_reduce_fusion.1
  257.1 6.3 convolution_bitcast_fusion.2
  263.5 25.8 %all-gather.11.cloned.1.call-done = bf16[4,1024,480]{1,2,0:T(8,128)(2,1)} async-done(((bf16[4,256,480]{1,2,0:T(8,128)(2,1)}), bf16[4,1024,480]{1,2,0:T(8,128)(2,1)}) %all-gather.11.cloned.1.call-update) | async-done | bytes 3932176 | tf_op jit(solution)/shard_map/all_gather | solution.py:162
  293.6 220.6 %while.31 = (s32[]{:T(128)}, f32[4,5,1024,24]{2,3,1,0:T(8,128)}, f32[4,5,1024,24]{2,3,1,0:T(8,128)}, f32[4,5,1024,24]{2,3,1,0:T(8,128)}, s32[4]{0:T(128)S(1)}, /...) while((s32[]{:T(128)}, f32[4,5,1024,24]{2,3,1,0:T(8,128)}, ...), condition=%wide.region_13.14_spmd.clone.clone, body=%wide.region_11.13_spmd.clone.sunk.clone | while | flops 1321201664 | bytes 244520096 | solution.py:196
  299.6 7.2 copy-done.1
  312.9 14.5 %multiply_reduce_fusion.8 = (f32[5,1024]{1,0:T(8,128)S(1)}, f32[5,1024,1024]{1,2,0:T(8,128)}) fusion(f32[5,1024,1024]{1,2,0:T(8,128)} %copy-done.1, f32[5,1024]{1,0:T(8,128)S(1)} %dynamic-slice_bitcast_fusion.3, pred[1024]{0:T(1024)(128)(4,1)S(1)} %iota_compare_fusion.7, bf16[4,5,1024,24]{2,3,1,0:T(8,128)(2,1)} %get-tuple-element.508, ...), kind=kOutput, calls=%fused_computation.22.clone.1.clone | convolution fusion | flops 272624640 | bytes 42477568 | tf_op jit(solution)/shard_map/while/body/eval_jaxpr/hqd,hkd->hqk/dot_general | solution.py:183
  327.5 14.9 %multiply_convert_fusion.4 = bf16[5,1024,1024]{1,2,0:T(8,128)(2,1)S(1)} fusion(f32[5,1024,1024]{1,2,0:T(8,128)} %get-tuple-element.445, f32[5,1024,1024]{1,2,0:T(8,128)} %copy-done.1, f32[5,1024]{1,0:T(8,128)S(1)} %get-tuple-element.446, f32[5,1024]{1,0:T(8,128)S(1)} %dynamic-slice_bitcast_fusion.3, pred[1024]{0:T(1024)(128)(4,1)S(1)} %iota_compare_fusion.7), kind=kLoop, calls=%fused_computation.21.clone.1.clone | loop fusion | flops 26214400 | bytes 52470784 | tf_op jit(solution)/shard_map/while/body/eval_jaxpr/convert_element_type | solution.py:187
  355.2 7.0 copy-done.1
  362.2 6.1 fusion.179
  368.3 14.3 %multiply_reduce_fusion.8 = (f32[5,1024]{1,0:T(8,128)S(1)}, f32[5,1024,1024]{1,2,0:T(8,128)}) fusion(f32[5,1024,1024]{1,2,0:T(8,128)} %copy-done.1, f32[5,1024]{1,0:T(8,128)S(1)} %dynamic-slice_bitcast_fusion.3, pred[1024]{0:T(1024)(128)(4,1)S(1)} %iota_compare_fusion.7, bf16[4,5,1024,24]{2,3,1,0:T(8,128)(2,1)} %get-tuple-element.508, ...), kind=kOutput, calls=%fused_computation.22.clone.1.clone | convolution fusion | flops 272624640 | bytes 42477568 | tf_op jit(solution)/shard_map/while/body/eval_jaxpr/hqd,hkd->hqk/dot_general | solution.py:183
  382.5 14.8 %multiply_convert_fusion.4 = bf16[5,1024,1024]{1,2,0:T(8,128)(2,1)S(1)} fusion(f32[5,1024,1024]{1,2,0:T(8,128)} %get-tuple-element.445, f32[5,1024,1024]{1,2,0:T(8,128)} %copy-done.1, f32[5,1024]{1,0:T(8,128)S(1)} %get-tuple-element.446, f32[5,1024]{1,0:T(8,128)S(1)} %dynamic-slice_bitcast_fusion.3, pred[1024]{0:T(1024)(128)(4,1)S(1)} %iota_compare_fusion.7), kind=kLoop, calls=%fused_computation.21.clone.1.clone | loop fusion | flops 26214400 | bytes 52470784 | tf_op jit(solution)/shard_map/while/body/eval_jaxpr/convert_element_type | solution.py:187
  410.1 7.0 copy-done.1
  423.2 14.3 %multiply_reduce_fusion.8 = (f32[5,1024]{1,0:T(8,128)S(1)}, f32[5,1024,1024]{1,2,0:T(8,128)}) fusion(f32[5,1024,1024]{1,2,0:T(8,128)} %copy-done.1, f32[5,1024]{1,0:T(8,128)S(1)} %dynamic-slice_bitcast_fusion.3, pred[1024]{0:T(1024)(128)(4,1)S(1)} %iota_compare_fusion.7, bf16[4,5,1024,24]{2,3,1,0:T(8,128)(2,1)} %get-tuple-element.508, ...), kind=kOutput, calls=%fused_computation.22.clone.1.clone | convolution fusion | flops 272624640 | bytes 42477568 | tf_op jit(solution)/shard_map/while/body/eval_jaxpr/hqd,hkd->hqk/dot_general | solution.py:183
  437.5 14.8 %multiply_convert_fusion.4 = bf16[5,1024,1024]{1,2,0:T(8,128)(2,1)S(1)} fusion(f32[5,1024,1024]{1,2,0:T(8,128)} %get-tuple-element.445, f32[5,1024,1024]{1,2,0:T(8,128)} %copy-done.1, f32[5,1024]{1,0:T(8,128)S(1)} %get-tuple-element.446, f32[5,1024]{1,0:T(8,128)S(1)} %dynamic-slice_bitcast_fusion.3, pred[1024]{0:T(1024)(128)(4,1)S(1)} %iota_compare_fusion.7), kind=kLoop, calls=%fused_computation.21.clone.1.clone | loop fusion | flops 26214400 | bytes 52470784 | tf_op jit(solution)/shard_map/while/body/eval_jaxpr/convert_element_type | solution.py:187
  465.0 7.0 copy-done.1
  478.1 14.3 %multiply_reduce_fusion.8 = (f32[5,1024]{1,0:T(8,128)S(1)}, f32[5,1024,1024]{1,2,0:T(8,128)}) fusion(f32[5,1024,1024]{1,2,0:T(8,128)} %copy-done.1, f32[5,1024]{1,0:T(8,128)S(1)} %dynamic-slice_bitcast_fusion.3, pred[1024]{0:T(1024)(128)(4,1)S(1)} %iota_compare_fusion.7, bf16[4,5,1024,24]{2,3,1,0:T(8,128)(2,1)} %get-tuple-element.508, ...), kind=kOutput, calls=%fused_computation.22.clone.1.clone | convolution fusion | flops 272624640 | bytes 42477568 | tf_op jit(solution)/shard_map/while/body/eval_jaxpr/hqd,hkd->hqk/dot_general | solution.py:183
  492.3 14.8 %multiply_convert_fusion.4 = bf16[5,1024,1024]{1,2,0:T(8,128)(2,1)S(1)} fusion(f32[5,1024,1024]{1,2,0:T(8,128)} %get-tuple-element.445, f32[5,1024,1024]{1,2,0:T(8,128)} %copy-done.1, f32[5,1024]{1,0:T(8,128)S(1)} %get-tuple-element.446, f32[5,1024]{1,0:T(8,128)S(1)} %dynamic-slice_bitcast_fusion.3, pred[1024]{0:T(1024)(128)(4,1)S(1)} %iota_compare_fusion.7), kind=kLoop, calls=%fused_computation.21.clone.1.clone | loop fusion | flops 26214400 | bytes 52470784 | tf_op jit(solution)/shard_map/while/body/eval_jaxpr/convert_element_type | solution.py:187
  530.3 7.0 convolution_bitcast_fusion.3
  539.5 7.0 convolution_bitcast_fusion.4
  547.2 6.7 add_convert_fusion
  554.4 21.9 %psum.73 = f32[3,120]{1,0:T(4,128)} all-reduce(f32[3,120]{1,0:T(4,128)S(1)} %reduce_sum.175), channel_id=1, replica_groups=mesh['dp'=8,'tensor'=4] {'dp'}, use_global_device_ids=true, to_apply=%region_23.24 | all-reduce | flops 360 | bytes 2880 | tf_op jit(solution)/shard_map/psum | solution.py:223
  576.3 31.3 %all-reduce.4.cloned.1.call-done = (f32[3,480,120]{1,2,0:T(8,128)}, f32[120,480]{1,0:T(8,128)}) async-done(((f32[3,480,120]{1,2,0:T(8,128)}, f32[120,480]{1,0:T(8,128)}), (f32[3,480,120]{1,2,0:T(8,128)}, f32[120,480]{1,0:T(8,128)})) %all-reduce.4.cloned.1.call-update) | async-done | bytes 921616 | tf_op jit(solution)/shard_map/psum | solution.py:223
  609.9 84.8 %reduce-scatter.19.cloned.1.call-done = f32[240,480]{1,0:T(8,128)} async-done(((f32[1920,480]{1,0:T(8,128)}), f32[240,480]{1,0:T(8,128)}) %reduce-scatter.19.cloned.1.call-update) | async-done | bytes 460816
  696.7 22.2 %reduce-scatter.21.cloned.1.call-done = f32[120,240]{1,0:T(8,128)} async-done(((f32[480,240]{1,0:T(8,128)}), f32[120,240]{1,0:T(8,128)}) %reduce-scatter.21.cloned.1.call-update) | async-done | bytes 115216
  720.6 69.8 %reduce-scatter.13.cloned.1.call-done = f32[4,256,480]{1,2,0:T(8,128)} async-done(((f32[4,1024,480]{1,2,0:T(8,128)}), f32[4,256,480]{1,2,0:T(8,128)}) %reduce-scatter.13.cloned.1.call-update) | async-done | bytes 1966096 | tf_op jit(solution)/shard_map/reduce_scatter | solution.py:217
  792.8 39.9 %all-reduce = (f32[480]{0:T(512)}, f32[480]{0:T(512)}, f32[480]{0:T(512)}, f32[480]{0:T(512)}, f32[480]{0:T(512)}, /*index=5*/f32[1920]{0:T(1024)}, f32[480]{0:T(512)}) all-reduce(f32[480]{0:T(512)S(1)} %get-tuple-element.219, f32[480]{0:T(512)S(1)} %get-tuple-element.224, ...), channel_id=1, replica_groups=mesh['dp'=8,'tensor'=4] {'dp','tensor'}, use_global_device_ids=true, to_apply=%region_18.19 | all-reduce | flops 4800 | bytes 38400 | tf_op jit(solution)/shard_map/psum | solution.py:234
  (234 shorter events, 223.8 us)
Async XLA Ops:
  8.0 42.5 %all-gather.5.cloned.1.call-start = ((), (), s32[]{:S(2)}) async-start(), calls=%async_computation.6 | async-start | bytes 4915200 | tf_op jit(solution)/shard_map/all_gather | solution.py:76
  14.1 185.9 %reduce-scatter.11.cloned.1.call-start = ((), (), s32[]{:S(2)}) async-start(), calls=%async_computation.7 | async-start | bytes 9830400 | tf_op jit(solution)/shard_map/reduce_scatter | solution.py:114
  14.7 43.1 %copy-start.17 = (f32[1024,24]{0,1:T(8,128)}, f32[1024,24]{0,1:T(8,128)S(1)}, u32[]{:S(2)}) copy-start(f32[1024,24]{0,1:T(8,128)S(1)} %get-tuple-element.293) | copy-start | bytes 294916
  14.7 43.1 %copy-start.19 = (f32[1024,24]{0,1:T(8,128)}, f32[1024,24]{0,1:T(8,128)S(1)}, u32[]{:S(2)}) copy-start(f32[1024,24]{0,1:T(8,128)S(1)} %get-tuple-element.295) | copy-start | bytes 294916
  60.1 65.2 %copy-start.21 = (bf16[120,480]{1,0:T(8,128)(2,1)S(1)}, bf16[120,480]{1,0:T(8,128)(2,1)}, u32[]{:S(2)}) copy-start(bf16[120,480]{1,0:T(8,128)(2,1)} %param.24) | copy-start | bytes 345604
  130.8 69.2 %copy-start.2 = (bf16[4,256,480]{1,2,0:T(8,128)(2,1)S(1)}, bf16[4,256,480]{1,2,0:T(8,128)(2,1)}, u32[]{:S(2)}) copy-start(bf16[4,256,480]{1,2,0:T(8,128)(2,1)} %param.19) | copy-start | bytes 2949124
  130.9 69.2 %copy-start.37 = (f32[480]{0:T(512)S(1)}, f32[480]{0:T(512)}, u32[]{:S(2)}) copy-start(f32[480]{0:T(512)} %param.25) | copy-start | bytes 5764
  130.9 74.2 %all-gather.7.cloned.1.call-start = ((), (), s32[]{:S(2)}) async-start(), calls=%async_computation.8 | async-start | bytes 2211840 | tf_op jit(solution)/shard_map/all_gather | solution.py:119
  138.3 97.3 %all-gather.9.cloned.1.call-start = ((), (), s32[]{:S(2)}) async-start(), calls=%async_computation.9 | async-start | bytes 2211840 | tf_op jit(solution)/shard_map/all_gather | solution.py:120
  138.4 66.7 %copy-start.33 = (f32[1920]{0:T(1024)S(1)}, f32[1920]{0:T(1024)}, u32[]{:S(2)}) copy-start(f32[1920]{0:T(1024)} %param.29) | copy-start | bytes 23044
  138.4 66.7 %copy-start.38 = (f32[480]{0:T(512)S(1)}, f32[480]{0:T(512)}, u32[]{:S(2)}) copy-start(f32[480]{0:T(512)} %param.26) | copy-start | bytes 5764
  138.5 66.7 %copy-start.45 = (f32[480]{0:T(512)S(1)}, f32[480]{0:T(512)}, u32[]{:S(2)}) copy-start(f32[480]{0:T(512)} %param.27) | copy-start | bytes 5764
  145.2 144.0 %all-gather.11.cloned.1.call-start = ((), (), s32[]{:S(2)}) async-start(), calls=%async_computation.10 | async-start | bytes 4915200 | tf_op jit(solution)/shard_map/all_gather | solution.py:162
  203.3 48.1 %copy-start.28 = (f32[4,256]{1,0:T(4,128)}, f32[4,256]{1,0:T(4,128)S(1)}, u32[]{:S(2)}) copy-start(f32[4,256]{1,0:T(4,128)S(1)} %broadcast_multiply_fusion.8) | copy-start | bytes 12292
  205.0 46.3 %copy-start.31 = (f32[4,256]{1,0:T(4,128)}, f32[4,256]{1,0:T(4,128)S(1)}, u32[]{:S(2)}) copy-start(f32[4,256]{1,0:T(4,128)S(1)} %add_rsqrt_fusion) | copy-start | bytes 12292
  257.1 280.4 %reduce-scatter.17.cloned.1.call-start = ((), (), s32[]{:S(2)}) async-start(), calls=%async_computation.13 | async-start | bytes 4423680 | tf_op jit(solution)/shard_map/reduce_scatter | solution.py:248
  263.4 344.2 %all-reduce.4.cloned.1.call-start = ((), (), s32[]{:S(2)}) async-start(), calls=%async_computation.16 | async-start | bytes 1966080 | tf_op jit(solution)/shard_map/psum | solution.py:223
  293.6 220.7 %copy-start.20 = (f32[1024,24]{0,1:T(8,128)S(1)}, f32[1024,24]{0,1:T(8,128)}, u32[]{:S(2)}) copy-start(f32[1024,24]{0,1:T(8,128)} %copy-done.19) | copy-start | bytes 294916
  530.2 164.5 %reduce-scatter.19.cloned.1.call-start = ((), (), s32[]{:S(2)}) async-start(), calls=%async_computation.14 | async-start | bytes 4423680
  537.3 181.6 %reduce-scatter.21.cloned.1.call-start = ((), (), s32[]{:S(2)}) async-start(), calls=%async_computation.15 | async-start | bytes 614400
  539.4 250.9 %reduce-scatter.13.cloned.1.call-start = ((), (), s32[]{:S(2)}) async-start(), calls=%async_computation.11 | async-start | bytes 9830400 | tf_op jit(solution)/shard_map/reduce_scatter | solution.py:217
  546.5 289.4 %reduce-scatter.15.cloned.1.call-start = ((), (), s32[]{:S(2)}) async-start(), calls=%async_computation.12 | async-start | bytes 614400 | tf_op jit(solution)/shard_map/reduce_scatter | solution.py:251
  553.9 236.5 %copy-start.3 = (bf16[4,256,480]{1,2,0:T(8,128)(2,1)S(1)}, bf16[4,256,480]{1,2,0:T(8,128)(2,1)}, u32[]{:S(2)}) copy-start(bf16[4,256,480]{1,2,0:T(8,128)(2,1)} %param.19) | copy-start | bytes 2949124
  553.9 236.5 %copy-start.23 = (f32[4,256]{1,0:T(4,128)S(1)}, f32[4,256]{1,0:T(4,128)}, u32[]{:S(2)}) copy-start(f32[4,256]{1,0:T(4,128)} %copy-done.22) | copy-start | bytes 12292
  553.9 236.5 %copy-start.25 = (f32[4,256]{1,0:T(4,128)S(1)}, f32[4,256]{1,0:T(4,128)}, u32[]{:S(2)}) copy-start(f32[4,256]{1,0:T(4,128)} %copy-done.24) | copy-start | bytes 12292
  553.9 236.5 %copy-start.30 = (f32[480]{0:T(512)S(1)}, f32[480]{0:T(512)}, u32[]{:S(2)}) copy-start(f32[480]{0:T(512)} %param.20) | copy-start | bytes 5764
  554.3 238.5 %copy-start.34 = (f32[480]{0:T(512)S(1)}, f32[480]{0:T(512)}, u32[]{:S(2)}) copy-start(f32[480]{0:T(512)} %get-tuple-element.268) | copy-start | bytes 5764
  554.3 238.5 %copy-start.35 = (f32[480]{0:T(512)S(1)}, f32[480]{0:T(512)}, u32[]{:S(2)}) copy-start(f32[480]{0:T(512)} %get-tuple-element.288) | copy-start | bytes 5764
  554.3 238.5 %copy-start.36 = (f32[1920]{0:T(1024)S(1)}, f32[1920]{0:T(1024)}, u32[]{:S(2)}) copy-start(f32[1920]{0:T(1024)} %get-tuple-element.298) | copy-start | bytes 23044
  554.3 238.5 %copy-start.40 = (f32[480]{0:T(512)S(1)}, f32[480]{0:T(512)}, u32[]{:S(2)}) copy-start(f32[480]{0:T(512)} %get-tuple-element.217) | copy-start | bytes 5764
  554.3 238.5 %copy-start.41 = (f32[480]{0:T(512)S(1)}, f32[480]{0:T(512)}, u32[]{:S(2)}) copy-start(f32[480]{0:T(512)} %get-tuple-element.223) | copy-start | bytes 5764
  554.3 278.4 %copy-start.7 = (f32[4,256,480]{1,2,0:T(8,128)S(1)}, f32[4,256,480]{1,2,0:T(8,128)}, u32[]{:S(2)}) copy-start(f32[4,256,480]{1,2,0:T(8,128)} %copy-done.6) | copy-start | bytes 5898244
  (32 other events, 209.7 us)
Sparse Core Ops, SparseCore 0:
  14.3 36.1 all-gather.4
  131.0 69.0 reduce-scatter.10
  257.2 32.0 all-gather.10
Sparse Core Ops, SparseCore 1:
  138.3 47.9 all-gather.6
  189.1 46.4 all-gather.8
  263.5 82.7 reduce-scatter.16
  530.3 77.3 all-reduce.3
  611.3 83.3 reduce-scatter.18
  697.9 20.9 reduce-scatter.20
  721.5 68.8 reduce-scatter.12
  793.4 21.3 reduce-scatter.14
where the time goes:
time: 852 us; the launch traced here: 845 us
  waiting for transfers between devices  325 us (38%)
  matrix products  234 us (27%)
  other arithmetic  134 us (16%)
  blocking collectives  73.4 us (9%)
  local copies, waits for them, and re-layouts  61.5 us (7%)
  between operations  16.1 us (2%)
    unnamed x13, waiting for transfers between devices  107 us
    reduce_scatter x1, waiting for transfers between devices, shards(): lax.psum_scatter(grad_normed_part, 'tensor', scatter_dimension=1, tiled=T...  69.8 us
    convert_element_type x4, other arithmetic, attend_back(): grad_scores = (probs_full * (grad_probs - inner_sum)).astype(jnp.bfloat16)  59.4 us
    dot_general x4, matrix products, attend_back(): jnp.einsum('hqd,hkd->hqk', grad_one, value_one, preferred_element_type=jn...  57.4 us
    reduce_scatter x1, waiting for transfers between devices, shards(): lax.psum_scatter(partial_branch, 'tensor', scatter_dimension=1, tiled=True)  54.4 us
    psum x1, blocking collectives, shards(): lax.psum((grad_attn_gain, grad_attn_shift, grad_out_bias, grad_ffn_gain,...  39.9 us
    all_gather x1, waiting for transfers between devices, shards(): lax.all_gather(first_normalized.astype(jnp.bfloat16), 'tensor', axis=1, t...  34.7 us
    dot_general x8, matrix products, masked_scores(): jnp.einsum('hqd,hkd->hqk', query_one, key_one, preferred_element_type=jnp...  32.7 us
  transfers between devices with their start and end apart: 11, of which 8 were waited for; matrix products, arithmetic and copies ran while one was open for 33% of the time, Pallas kernels for 0%

commit v1 on v0

v1 whole, which is shorter than its diff:
```python
import math

import jax
import jax.numpy as jnp
import numpy as np
from jax import lax
from jax.experimental import pallas as pl
from jax.experimental.pallas import tpu as pltpu
from jax.sharding import PartitionSpec as P

HEAD_DIM = 24
HEAD_ROWS = 32
EPS = 1e-05
MASK_FILL = -1000000000.0
LOG2E = math.log2(math.e)
SAFE_SCORE = 85.0
WORK_SCALE = 0.1
BLOCK = 256
LANES = 512
BF16 = jnp.bfloat16
F32 = jnp.float32

NN = (((1,), (0,)), ((), ()))
NT = (((1,), (1,)), ((), ()))
TN = (((0,), (0,)), ((), ()))


def product(left, right, dims=NN):
    return lax.dot_general(left, right, dims, preferred_element_type=F32)


def vmem(count):
    return [pl.BlockSpec(memory_space=pltpu.VMEM)] * count


def smem():
    return pl.BlockSpec(memory_space=pltpu.SMEM)


def hbm(count=1):
    return [pl.BlockSpec(memory_space=pltpu.HBM)] * count


def call(kernel, inputs, outs, scratch=(), in_specs=None, out_specs=None, limit=40, tiles=0):
    flops = int(2 * 256**3 * tiles * WORK_SCALE)
    in_specs = vmem(len(inputs)) if in_specs is None else in_specs
    inputs = [
        pltpu.with_memory_space_constraint(part, pltpu.HBM)
        if spec.memory_space is pltpu.HBM
        else part
        for part, spec in zip(inputs, in_specs)
    ]
    out_specs = vmem(len(outs)) if out_specs is None else out_specs
    outs = [
        pltpu.HBM(part.shape, part.dtype) if spec.memory_space is pltpu.HBM else part
        for part, spec in zip(outs, out_specs)
    ]
    return pl.pallas_call(
        kernel,
        out_shape=outs,
        in_specs=in_specs,
        out_specs=out_specs,
        scratch_shapes=list(scratch),
        compiler_params=pltpu.CompilerParams(vmem_limit_bytes=limit << 20),
        cost_estimate=pl.CostEstimate(flops=flops, transcendentals=0, bytes_accessed=0),
    )(*inputs)


def shape(dims, dtype):
    return jax.ShapeDtypeStruct(dims, dtype)


def at_block(index, size):
    return pl.ds(pl.multiple_of(index * size, size), size)


def split_three(values):
    high = values.astype(BF16).astype(F32)
    rest = values - high
    middle = rest.astype(BF16).astype(F32)
    return high, middle, rest - middle


def after(values, *others):
    return lax.optimization_barrier((values, *others))[0]


def norm_columns(values):
    centre = values - jnp.mean(values, axis=0, keepdims=True)
    inverse = lax.rsqrt(jnp.mean(centre * centre, axis=0, keepdims=True) + EPS)
    return centre * inverse, inverse


def norm_columns_back(upstream, unit, inverse, gain):
    scaled = upstream * gain
    centred = scaled - jnp.mean(scaled, axis=0, keepdims=True)
    return inverse * (centred - unit * jnp.mean(scaled * unit, axis=0, keepdims=True))


def pair_kernel(info, up, down, pair, up_inside, down_inside, semaphores):
    copies = [
        pltpu.make_async_copy(up, up_inside, semaphores.at[0]),
        pltpu.make_async_copy(down, down_inside, semaphores.at[1]),
    ]
    for copy in copies:
        copy.start()
    pair[...] = jnp.zeros_like(pair)
    for copy in copies:
        copy.wait()
    size = up.shape[1]
    up_half = up_inside[...]
    down_half = down_inside[...].astype(F32).T.astype(BF16)

    @pl.when(info[0] & 1 == 0)
    def _():
        pair[:, :size] = up_half
        pair[:, BLOCK : BLOCK + size] = down_half

    @pl.when(info[0] & 1 == 1)
    def _():
        pair[:, :size] = down_half
        pair[:, BLOCK : BLOCK + size] = up_half


def norm_kernel(
    hidden_in,
    gain,
    shift,
    out_weight_in,
    first_out,
    second_out,
    hidden,
    gain_inside,
    shift_inside,
    out_weight,
    rows_scratch,
    semaphores,
):
    rows, width, chunk = hidden.shape
    copies = [
        pltpu.make_async_copy(hidden_in.at[row], hidden.at[row], semaphores.at[row])
        for row in range(rows)
    ]
    others = [
        pltpu.make_async_copy(gain, gain_inside, semaphores.at[4]),
        pltpu.make_async_copy(shift, shift_inside, semaphores.at[5]),
        pltpu.make_async_copy(out_weight_in, out_weight, semaphores.at[6]),
    ]
    for copy in others[:2] + copies + others[2:]:
        copy.start()
    rows_scratch[...] = jnp.zeros_like(rows_scratch)
    others[0].wait()
    others[1].wait()
    rows_scratch[0:1, :] = gain_inside[...]
    rows_scratch[1:2, :] = shift_inside[...]
    columns = rows_scratch[...].T
    half = rows // 2
    for row in range(rows):
        copies[row].wait()
        unit, _ = norm_columns(hidden[row].astype(F32))
        target = first_out if row < half else second_out
        place = row % half * width
        target[place : place + width, :] = (unit * columns[:, 0:1] + columns[:, 1:2]).astype(
            BF16
        )
    others[2].wait()
    own = out_weight.shape[0]
    second_out[half * width : half * width + own, :] = out_weight[:, :chunk]
    rest = width - chunk
    second_out[half * width + own : half * width + 2 * own, :] = jnp.zeros((own, chunk), BF16)
    second_out[half * width + own : half * width + 2 * own, :rest] = out_weight[:, chunk:]


def prepare_kernel(heads, info, *refs):
    outside, refs = refs[:9], refs[9:]
    weight_out, weight_turned_out, columns_out, bias_out, up_bias_out, vector_rows = refs[:6]
    weight_scratch, bias_rows = refs[6:8]
    inside, semaphores = refs[8:17], refs[17]
    copies = [
        pltpu.make_async_copy(source, target, semaphores.at[place])
        for place, (source, target) in enumerate(zip(outside, inside))
    ]
    for copy in copies:
        copy.start()
    vectors, (up_bias, weight, bias) = inside[:6], inside[6:]
    width = weight.shape[1]
    vector_rows[...] = jnp.zeros_like(vector_rows)
    for copy in copies:
        copy.wait()
    for place, vector in enumerate(vectors):
        vector_rows[place : place + 1, :] = vector[...]
    columns_out[...] = jnp.concatenate([vector_rows[...], jnp.zeros((120, width), F32)]).T
    span = heads * HEAD_DIM
    for c in range(3):
        own = slice(c * span, (c + 1) * span)
        weight_scratch[own, :] = weight[c].astype(F32).T
        bias_out[own, :] = jnp.broadcast_to(bias[c : c + 1, :], (128, span)).T
    weight_out[...] = weight_scratch[...].astype(BF16)
    weight_turned_out[...] = weight_scratch[...].T.astype(BF16)
    bias_rows[...] = jnp.zeros_like(bias_rows)
    count = up_bias.shape[1]
    block = count // 8
    spread = jnp.broadcast_to(up_bias[...], (8, count))
    for j in range(8):
        moved = pltpu.roll(spread, lax.rem(count - (info[1] ^ j) * block, count), 1)
        bias_rows[j : j + 1, :block] = moved[0:1, :block]
    up_bias_out[...] = bias_rows[...].T


def assemble_kernel(chunks, info, *refs):
    parts, (out, rows) = refs[:chunks], refs[chunks:]
    size = parts[0].shape[0]
    for k in range(chunks):
        half = parts[k][:, (k & 1) * BLOCK : ((k & 1) + 1) * BLOCK]
        rows[at_block(info[0] ^ k, size), :] = half.astype(F32)
    out[...] = rows[...].astype(BF16)


def rotary_constants(chunk, chunks):
    half = HEAD_DIM // 2
    element = np.arange(HEAD_DIM)
    frequency = (1.0 / 10000.0 ** (np.arange(0, HEAD_DIM, 2).astype(np.float32) / HEAD_DIM)).astype(
        np.float32
    )
    per_row = frequency[element % half].astype(np.float64)
    inner = per_row[:, None] * np.arange(chunk)[None, :]
    outer = per_row[:, None] * (np.arange(chunks) * chunk)[None, :]
    outer = np.repeat(outer[:, :, None], chunk, axis=2).transpose(1, 0, 2)
    inner_pair = np.stack([np.cos(inner), np.sin(inner)]).astype(np.float32)
    outer_pair = np.stack([np.cos(outer), np.sin(outer)]).astype(np.float32)
    return inner_pair, outer_pair


def chunk_tables(inner, outer, index):
    cos_in, sin_in = inner[0], inner[1]
    cos_out, sin_out = outer[0, index], outer[1, index]
    element = lax.broadcasted_iota(jnp.int32, cos_in.shape, 0)
    sine = sin_in * cos_out + cos_in * sin_out
    return cos_in * cos_out - sin_in * sin_out, jnp.where(
        element < HEAD_DIM // 2, -sine, sine
    )


def swap_halves(values):
    return pltpu.roll(values, HEAD_DIM // 2, 0)


def attend_kernel(heads, chunks, chunk, first_row, rows, info, lengths, *refs):
    parts = refs[:chunks]
    weight, bias, inner, outer, own_out, near_out, cross_out = refs[chunks : chunks + 7]
    queries, keys, values, logsum, mixed_turned, normed_out, key_rows, peak, flat = refs[
        chunks + 7 : chunks + 16
    ]
    normed, semaphores = refs[chunks + 16 :]
    position = info[0]
    width = normed.shape[1]
    full = chunk * chunks
    span = heads * HEAD_DIM
    scale = LOG2E * HEAD_DIM**-0.5
    blocks_full = full // BLOCK

    def one_row(r, carry):
        length = lengths[first_row + r]
        for k in range(chunks):
            normed[r, :, at_block(position ^ k, chunk)] = parts[k][at_block(r, width), :]
        pltpu.make_async_copy(normed.at[r], normed_out.at[r], semaphores.at[r]).start()
        flat[...] = product(weight[...], normed[r])
        line = lax.broadcasted_iota(jnp.int32, (8, chunk), 0)
        ones = jnp.where(line < 3, 1.0, 0.0)
        query_line = jnp.where(line == 3, 1.0, 0.0)
        query_top = [jnp.zeros((1, chunk), F32) for _ in range(heads)]
        key_top = [jnp.zeros((1, chunk), F32) for _ in range(heads)]
        for j in range(chunks):
            at = slice(j * chunk, (j + 1) * chunk)
            cosine, sine = chunk_tables(inner, outer, j)
            query_cosine, query_sine = cosine * scale, sine * scale
            place = lax.broadcasted_iota(jnp.int32, (8, chunk), 1) + j * chunk
            key_line = jnp.where((line == 3) & (place >= length), MASK_FILL, ones)
            for h in range(heads):
                here = h * HEAD_DIM
                query, key, value = (
                    flat[c * span + here : c * span + here + HEAD_DIM, at]
                    + jnp.concatenate(
                        [bias[c * span + here : c * span + here + HEAD_DIM, :]] * (chunk // 128),
                        axis=1,
                    )
                    for c in range(3)
                )
                query = query * query_cosine + swap_halves(query) * query_sine
                key = key * cosine + swap_halves(key) * sine
                query_top[h] = jnp.maximum(
                    query_top[h], jnp.sum(query * query, axis=0, keepdims=True)
                )
                key_top[h] = jnp.maximum(key_top[h], jnp.sum(key * key, axis=0, keepdims=True))
                key_full = jnp.concatenate([key, key_line])
                queries[r, h, :, at] = jnp.concatenate([query, query_line]).astype(BF16)
                keys[r, h, :, at] = key_full.astype(BF16)
                values[r, h, :, at] = jnp.concatenate([value, ones]).astype(BF16)
                key_rows[h, at, :] = key_full.T.astype(BF16)
        bound = jnp.zeros((1, 1), F32)
        for h in range(heads):
            bound = jnp.maximum(
                bound,
                jnp.max(query_top[h], axis=-1, keepdims=True)
                * jnp.max(key_top[h], axis=-1, keepdims=True),
            )
        safe = jnp.max(bound) <= SAFE_SCORE * SAFE_SCORE
        peak[...] = jnp.zeros_like(peak)

        @pl.when(jnp.logical_not(safe))
        def _():
            def one_head(h, carry):
                scores = product(key_rows[h], queries[r, h])
                peak[pl.ds(h, 1), :] = (
                    jnp.max(scores, axis=0, keepdims=True).astype(BF16).astype(F32)
                )
                return carry

            lax.fori_loop(0, heads, one_head, 0)

        head_line = lax.broadcasted_iota(jnp.int32, (HEAD_ROWS, full), 0)

        def with_keys(count):
            def one_head(h, carry):
                top = peak[pl.ds(h, 1), :]
                query = jnp.where(
                    head_line == HEAD_DIM, -top, queries[r, h].astype(F32)
                ).astype(BF16)
                exponent = jnp.exp2(product(key_rows[h, :count, :], query)).astype(BF16)
                blend = product(values[r, h, :, :count], exponent)
                total = blend[HEAD_DIM : HEAD_DIM + 1, :]
                logsum[r, pl.ds(h, 1), :] = top + jnp.log2(total)
                mixed_turned[r, pl.ds(pl.multiple_of(h * HEAD_DIM, 8), HEAD_DIM), :] = blend[
                    :HEAD_DIM
                ] * (1.0 / total)
                return carry

            lax.fori_loop(0, heads, one_head, 0)

        blocks = (length + BLOCK - 1) // BLOCK
        for b in range(1, blocks_full + 1):
            pl.when(blocks == b)(lambda b=b: with_keys(b * BLOCK))
        mixed_turned[r, span:, :] = jnp.zeros((mixed_turned.shape[1] - span, full), F32)
        own_out[r] = mixed_turned[r, :, at_block(position, chunk)].astype(BF16)
        near_out[r] = mixed_turned[r, :, at_block(position ^ 1, chunk)].astype(BF16)
        cross_out[r, 0] = mixed_turned[r, :, at_block(position ^ 2, chunk)].astype(BF16)
        cross_out[r, 1] = mixed_turned[r, :, at_block(position ^ 3, chunk)].astype(BF16)
        return carry

    lax.fori_loop(0, rows, one_row, 0)
    for r in range(rows):
        pltpu.make_async_copy(normed.at[r], normed_out.at[r], semaphores.at[r]).wait()


def attend_back_kernel(heads, chunks, chunk, row, local, first, last, info, lengths, *refs):
    upstream_own, upstream_near, upstream_cross, upstream_far = refs[:4]
    queries, keys, values, logsum, mixed_turned, normed_in, weight_turned, inner, outer = refs[
        4:13
    ]
    refs = refs[13:]
    if not first:
        carried = refs[0]
        refs = refs[1:]
    if last:
        out_own, out_near, out_cross, weight, vector_rows = refs[:5]
        refs = refs[5:]
    own_out, near_out, cross_out = refs[:3]
    refs = refs[3:]
    if last:
        even_pieces, odd_pieces, norm_sums = refs[:3]
        refs = refs[3:]
    else:
        running = refs[0]
        refs = refs[1:]
    (
        upstream,
        query_full,
        upstream_full,
        key_rows,
        value_rows,
        grads,
        grad_low,
        packed,
        normed,
        semaphore,
    ) = refs
    fetch = pltpu.make_async_copy(normed_in.at[local], normed, semaphore)
    fetch.start()
    position, index, length = info[0], info[1], lengths[row]
    full = chunk * chunks
    span = heads * HEAD_DIM
    upstream[:, at_block(position, chunk)] = upstream_own[local]
    upstream[:, at_block(position ^ 1, chunk)] = upstream_near[local]
    upstream[:, at_block(position ^ 2, chunk)] = upstream_cross[local, 0]
    upstream[:, at_block(position ^ 3, chunk)] = upstream_far[local, 1]
    zeros = jnp.zeros((5, chunk), F32)
    line = lax.broadcasted_iota(jnp.int32, (8, chunk), 0)
    for j in range(chunks):
        at = slice(j * chunk, (j + 1) * chunk)
        turned = upstream[:, at].astype(F32)
        blend = turned * mixed_turned[local, :, at]
        for h in range(heads):
            own = slice(h * HEAD_DIM, (h + 1) * HEAD_DIM)
            high, middle, rest = split_three(-jnp.sum(blend[own], axis=0, keepdims=True))
            extra = jnp.where(
                line == 0, high, jnp.where(line == 1, middle, jnp.where(line == 2, rest, 0.0))
            )
            upstream_full[h, :, at] = jnp.concatenate([turned[own], extra]).astype(BF16)
            high, middle, rest = split_three(-logsum[local, h : h + 1, at])
            extra = jnp.where(
                line == 0,
                high,
                jnp.where(
                    line == 1, middle, jnp.where(line == 2, rest, jnp.where(line == 3, 1.0, 0.0))
                ),
            )
            query = queries[local, h, :, at].astype(F32)[:HEAD_DIM]
            query_full[h, :, at] = jnp.concatenate([query, extra]).astype(BF16)
            key_rows[h, at, :] = keys[local, h, :, at].astype(F32).T.astype(BF16)
            value_rows[h, at, :] = values[local, h, :, at].astype(F32).T.astype(BF16)

    def with_keys(count):
        def one_head(h, carry):
            own = pl.ds(pl.multiple_of(h * HEAD_DIM, 8), HEAD_DIM)
            grad_query = jnp.zeros((HEAD_ROWS, full), F32)
            for b in range(count // BLOCK):
                at = slice(b * BLOCK, (b + 1) * BLOCK)
                probs = jnp.exp2(product(key_rows[h, at, :], query_full[h])).astype(BF16)
                grad_probs = product(value_rows[h, at, :], upstream_full[h]).astype(BF16)
                grad_scores = probs * grad_probs
                grads[2, own, at] = product(upstream_full[h], probs, NT)[:HEAD_DIM]
                grads[1, own, at] = product(query_full[h], grad_scores, NT)[:HEAD_DIM]
                grad_query += product(keys[local, h, :, at], grad_scores)
            grads[0, own, :] = grad_query[:HEAD_DIM]
            return carry

        lax.fori_loop(0, heads, one_head, 0)
        if count < full:
            grads[1, :, count:] = jnp.zeros((span, full - count), F32)
            grads[2, :, count:] = jnp.zeros((span, full - count), F32)

    blocks = (length + BLOCK - 1) // BLOCK
    for b in range(1, full // BLOCK + 1):
        pl.when(blocks == b)(lambda b=b: with_keys(b * BLOCK))

    sums = [[jnp.zeros((HEAD_DIM, 128), F32) for _ in range(heads)] for _ in range(3)]
    for j in range(chunks):
        at = slice(j * chunk, (j + 1) * chunk)
        cosine, sine = chunk_tables(inner, outer, j)
        query_cosine, query_sine = cosine * HEAD_DIM**-0.5, sine * HEAD_DIM**-0.5
        key_cosine, key_sine = cosine * (1.0 / LOG2E), sine * (1.0 / LOG2E)
        for h in range(heads):
            own = slice(h * HEAD_DIM, (h + 1) * HEAD_DIM)
            query, key, value = (grads[c, own, at] for c in range(3))
            query = query * query_cosine - swap_halves(query) * query_sine
            key = key * key_cosine - swap_halves(key) * key_sine
            for c, part in enumerate((query, key, value)):
                for piece in range(chunk // 128):
                    sums[c][h] = sums[c][h] + part[:, piece * 128 : (piece + 1) * 128]
                grads[c, own, at] = part
    for c in range(3):
        grad_low[c * span : (c + 1) * span, :] = grads[c].astype(BF16)
    for k in range(chunks):
        result = product(
            weight_turned[...], grad_low[:, at_block(position ^ k, chunk)]
        ).astype(BF16)
        if k == 0:
            own_out[...] = result
        elif k == 2:
            cross_out[...] = result
        else:
            near_out[k // 2] = result
    width = weight_turned.shape[0]
    fetch.wait()
    result = product(grad_low[...], normed[...], NT)
    bias_grad = jnp.concatenate(
        [jnp.sum(part, axis=1, keepdims=True) for group in sums for part in group]
    )
    bias_grad = jnp.broadcast_to(bias_grad, (3 * span, 128))
    if not first:
        result = result + carried[:, :width]
        bias_grad = bias_grad + carried[:, LANES:]
    if not last:
        running[:, :width] = result
        running[:, LANES:] = bias_grad
        return
    packed[: 3 * span, :width] = result
    gain_sum = jnp.zeros((8, width), F32)
    shift_sum = jnp.zeros((8, width), F32)
    gain, shift = vector_rows[0:1, :], vector_rows[1:2, :]
    for place in range(0, 3 * span, 8):
        own = slice(place, place + 8)
        factor = weight[own, :].astype(F32)
        column = bias_grad[own, 0:1]
        gain_sum = gain_sum + factor * (result[own] - shift * column)
        shift_sum = shift_sum + factor * column
    norm_sums[...] = jnp.zeros_like(norm_sums)
    norm_sums[0:1, :] = jnp.sum(gain_sum, axis=0, keepdims=True) / gain
    norm_sums[1:2, :] = jnp.sum(shift_sum, axis=0, keepdims=True)
    lane = lax.broadcasted_iota(jnp.int32, (3 * span, 128), 1)
    packed[: 3 * span, LANES - 128 :] = jnp.where(
        lane >= width - (LANES - 128), bias_grad, packed[: 3 * span, LANES - 128 :]
    )
    shared = (out_own[...].astype(F32) + out_near[0].astype(F32)) + out_cross[...].astype(F32)
    packed[3 * span : 4 * span, :] = shared[:span]
    packed[4 * span : 4 * span + 16, :] = shared[128:144]
    packed[4 * span + 16 :, :] = jnp.zeros((packed.shape[0] - 4 * span - 16, LANES), F32)
    size = packed.shape[0] // 8
    for j in range(8):
        target = odd_pieces if j % 2 else even_pieces
        target[j // 2] = packed[at_block(index ^ j, size), :].astype(BF16)


def gelu_parts(values):
    magnitude = jnp.abs(values) * (0.5**0.5)
    density = jnp.exp2(values * values * (-0.5 * LOG2E))
    step = 1.0 / (1.0 + 0.3275911 * magnitude)
    series = 1.061405429 * step - 1.453152027
    series = series * step + 1.421413741
    series = series * step - 0.284496736
    series = series * step + 0.254829592
    tail = 0.5 * series * step * density
    share = jnp.where(values < 0, tail, 1.0 - tail)
    return share, density * (1.0 / math.sqrt(2.0 * math.pi))


def feed_kernel(chunks, blocks, first_row, rows, last, info, *refs):
    hidden, cotangent, columns, up_bias = refs[:4]
    mixed_own, mixed_near, mixed_cross, mixed_far = refs[4:8]
    out_weight = refs[8 : 8 + chunks]
    refs = refs[8 + chunks :]
    if last:
        weights, carried, out_carried, sums_carried, bias_carried, hidden_before = refs[:6]
        refs = refs[6:]
    else:
        feeds, refs = refs[:12], refs[12:]
    hidden_out, grad_middle_out, grad_own, grad_near, grad_cross = refs[:5]
    refs = refs[5:]
    if last:
        kept_out, sent_out, out_own, out_near, out_cross = refs[:5]
    else:
        weights, carried, out_carried, sums_carried, bias_carried = refs[:5]
    refs = refs[5:]
    (
        out_rows,
        mixed,
        source,
        given,
        low_rows,
        down_total,
        back_total,
        bias_total,
        semaphores,
    ) = refs
    core, index = info[0] & 1, info[1]
    width, chunk = hidden.shape[1:]
    tokens = rows * chunk
    columns_held = mixed_own.shape[1]
    if not last:
        copies = []
        for side in range(2):
            sources = list(feeds[6 * side : 6 * side + 4])
            duo, duo_beside = feeds[6 * side + 4 : 6 * side + 6]
            place = core if side == 0 else 1 - core
            for e in range(2):
                sources += [duo.at[e], duo_beside.at[e]]
            for j in range(blocks):
                copies.append(
                    pltpu.make_async_copy(
                        sources[j], weights.at[place, j], semaphores.at[side, j]
                    )
                )
        for copy in copies:
            copy.start()
    own_rows = (out_weight[0].shape[0] - 2 * width) // 2
    for k in range(chunks):
        base = 2 * width
        out_rows[k] = jnp.zeros(out_rows.shape[1:], BF16)
        out_rows[k, :own_rows, :chunk] = out_weight[k][base : base + own_rows, :]
        out_rows[k, :own_rows, chunk:] = out_weight[k][
            base + own_rows : base + 2 * own_rows, : width - chunk
        ]
    for r in range(rows):
        at = slice(r * chunk, (r + 1) * chunk)
        mixed[0, :, at] = mixed_own[r]
        mixed[1, :, at] = mixed_near[r]
        mixed[2, :, at] = mixed_cross[r, 0]
        mixed[3, :, at] = mixed_far[r, 1]
        source[:, at] = hidden[first_row + r].astype(F32)
        given[:, at] = cotangent[first_row + r]
    middle = source[...] + columns[:, 2:3]
    for k in range(chunks):
        middle = middle + product(out_rows[k], mixed[k], TN)
    source[...] = middle
    unit, inverse = norm_columns(middle)
    low_rows[...] = (unit * columns[:, 3:4] + columns[:, 4:5]).astype(BF16)
    down_total[...] = middle + columns[:, 5:6]
    back_total[...] = jnp.zeros_like(back_total)
    bias_total[...] = jnp.zeros_like(bias_total)
    lane = lax.broadcasted_iota(jnp.int32, (BLOCK, 128), 1)
    if not last:
        for copy in copies:
            copy.wait()

    def one_block(j, carry):
        up_weight, down_weight = weights[0, j], weights[1, j]
        bias = jnp.sum(jnp.where(lane == j, up_bias[...], 0.0), axis=1, keepdims=True)
        upward = product(up_weight, low_rows[...], TN) + bias
        share, density = gelu_parts(upward)
        active = (upward * share).astype(BF16)
        down_total[...] += product(down_weight, active)
        grad_up = product(down_weight, given[...], TN) * (share + upward * density)
        bias_total[...] += jnp.where(lane == j, jnp.sum(grad_up, axis=1, keepdims=True), 0.0)
        grad_low = grad_up.astype(BF16)
        back_total[...] += product(up_weight, grad_low)
        up_grad = product(low_rows[...], grad_low, NT)
        down_grad = product(given[...], active, NT)
        if last:
            up_grad = (up_grad + carried[0, j]).astype(BF16)
            down_grad = (down_grad + carried[1, j]).astype(BF16)
            odd, place = j & 1, j >> 1

            @pl.when(core == 0)
            def _():
                kept_out[odd, place] = up_grad
                sent_out[odd, place] = down_grad

            @pl.when(core == 1)
            def _():
                kept_out[odd, place] = down_grad
                sent_out[odd, place] = up_grad
        else:
            carried[0, j] = up_grad
            carried[1, j] = down_grad
        return carry

    lax.fori_loop(0, blocks, one_block, 0)
    shift = first_row if last else 0
    if last:
        hidden_out[:first_row] = hidden_before[...]
    for r in range(rows):
        hidden_out[shift + r] = down_total[:, r * chunk : (r + 1) * chunk].astype(BF16)
    unit, inverse = norm_columns(source[...])
    back = back_total[...]
    given_wide = given[...].astype(F32)
    grad_middle = given_wide + norm_columns_back(back, unit, inverse, columns[:, 3:4])
    for r in range(rows):
        grad_middle_out[r] = grad_middle[:, r * chunk : (r + 1) * chunk]
    column_lane = lax.broadcasted_iota(jnp.int32, (width, 128), 1)
    totals = jnp.zeros((width, 128), F32)
    for place, values in enumerate((back * unit, back, grad_middle, given_wide)):
        totals = jnp.where(column_lane == place, jnp.sum(values, axis=1, keepdims=True), totals)
    branch = grad_middle.astype(BF16)
    targets = (out_own, out_near.at[0], out_cross, out_near.at[1]) if last else (None,) * 4
    for k in range(chunks):
        grad = product(out_rows[k], branch).astype(BF16)
        for r in range(rows):
            own = grad[:, r * chunk : (r + 1) * chunk]
            if k == 0:
                grad_own[r] = own
            elif k == 1:
                grad_near[r] = own
            else:
                grad_cross[r, k - 2] = own
        out_part = product(mixed[k], branch, NT)
        if last:
            targets[k][:columns_held, 384:] = jnp.zeros((columns_held, LANES - 384), BF16)
            targets[k][:columns_held, :width] = (out_part + out_carried[k]).astype(BF16)
        else:
            out_carried[k] = out_part
    if last:
        totals = (totals + sums_carried[...]).T
        bias_rows = (bias_total[...] + bias_carried[...]).T
        down_total[0:16, :] = jnp.zeros((16, tokens), F32)
        down_total[0:4, :width] = totals[:4]
        for j in range(blocks):
            down_total[pl.ds(4 + (index ^ j), 1), :BLOCK] = bias_rows[j : j + 1, :]
        for k in range(chunks):
            targets[k][columns_held:, :] = down_total[0:16, :LANES].astype(BF16)
    else:
        sums_carried[...] = totals
        bias_carried[...] = bias_total[...]


def norm_back_kernel(rows, hidden, columns, *refs):
    middle_grads, refs = refs[:2], refs[2:]
    own_parts, near_parts = refs[0 : 2 * rows : 2], refs[1 : 2 * rows : 2]
    cross_parts, (out,) = refs[2 * rows : 3 * rows - 1], refs[3 * rows - 1 :]
    cross_parts = list(cross_parts[:-1]) + [cross_parts[-1].at[0], cross_parts[-1].at[1]]
    gain = columns[:, 0:1]
    for row in range(rows):
        unit, inverse = norm_columns(hidden[row].astype(F32))
        grad = (
            own_parts[row][...].astype(F32)
            + near_parts[row][0].astype(F32)
            + cross_parts[row][...].astype(F32)
        )
        half = rows // 2
        result = middle_grads[row // half][row % half] + norm_columns_back(
            grad, unit, inverse, gain
        )
        out[row] = result.astype(BF16)


def add_pieces_kernel(even, beside, *outs):
    for i, out in enumerate(outs):
        out[...] = (even[i].astype(F32) + beside[i].astype(F32)).astype(BF16)


def own_piece_kernel(first, second, fourth, sixth, norm_sums, out):
    size = first.shape[0]
    total = first[...].astype(F32) + second[...].astype(F32)
    total = total + fourth[...].astype(F32) + sixth[...].astype(F32)
    out[:size, :] = total.astype(BF16)
    width = norm_sums.shape[1]
    values = norm_sums[...]
    high = values.astype(BF16)
    rest = (values - high.astype(F32)).astype(BF16)
    out[size:, 384:] = jnp.zeros((16, LANES - 384), BF16)
    out[size:, :width] = jnp.concatenate([high.astype(F32), rest.astype(F32)]).astype(BF16)


def feed_sum_kernel(info, first, second, fourth, sixth, keep, send, rows):
    total = first[...].astype(F32) + second[...].astype(F32)
    rows[...] = total + fourth[...].astype(F32) + sixth[...].astype(F32)
    size = keep.shape[0]
    chip = info[0] >> 1
    keep[...] = rows[at_block(chip, size), :].astype(BF16)
    send[...] = rows[at_block(1 - chip, size), :].astype(BF16)


def feed_pair_kernel(info, kept, came, mine, other, rows):
    rows[...] = kept[...].astype(F32) + came[...].astype(F32)
    size = mine.shape[0]
    core = info[0] & 1
    mine[...] = rows[at_block(core, size), :].astype(BF16)
    other[...] = rows[at_block(1 - core, size), :].astype(BF16)


def unpack_kernel(info, *refs):
    evens, beside = refs[:4], refs[4]
    refs = refs[5:]
    if len(refs) > 12:
        mine, came, refs = refs[0], refs[1], refs[2:]
        up_grad, down_grad = refs[10:12]
        refs = refs[:10] + refs[12:]
        count = up_grad.shape[1]

        def write(up, down):
            up_grad[...] = up[:, :count].astype(F32)
            down_grad[...] = down[...].astype(F32).T[:count, :]

        pl.when(info[0] & 1 == 0)(lambda: write(mine, came))
        pl.when(info[0] & 1 == 1)(lambda: write(came, mine))
    weight_grad, bias_grad, out_grad, gain, shift, out_bias, down_bias, up_bias = refs[:8]
    norm_gain, norm_shift, whole, line = refs[8:]
    size = whole.shape[0] // 8
    width = weight_grad.shape[1]
    norms = [evens[0][size:, :].astype(F32) + beside[0, size:, :].astype(F32)]
    for i in range(4):
        whole[at_block(info[1] ^ (2 * i), size), :] = evens[i][:size, :].astype(F32)
        whole[at_block(info[1] ^ (2 * i + 1), size), :] = beside[i, :size, :].astype(F32)
        if i > 0:
            norms.append(evens[i][size:, :].astype(F32) + beside[i, size:, :].astype(F32))
    norms = (norms[0] + norms[1]) + (norms[2] + norms[3])
    norms = norms[:8] + norms[8:16]
    norm_gain[...] = norms[0:1, :width]
    norm_shift[...] = norms[1:2, :width]
    columns = weight_grad.shape[2]
    for c in range(3):
        turned = whole[c * columns : (c + 1) * columns, :].T
        weight_grad[c] = turned[:width, :]
        bias_grad[c : c + 1, :] = turned[width : width + 1, :]
    out_grad[...] = whole[3 * columns : 4 * columns, :width]
    for place, target in enumerate((gain, shift, out_bias, down_bias)):
        target[...] = whole[4 * columns + place : 4 * columns + place + 1, :width]
    block = up_bias.shape[0] // 8
    for j in range(8):
        line[:, j * block : (j + 1) * block] = whole[
            4 * columns + 4 + j : 4 * columns + 5 + j, :block
        ]
    up_bias[...] = line[0, :]


def swap(values, axis, bit):
    size = lax.axis_size(axis)
    return lax.ppermute(values, axis, [(i, i ^ bit) for i in range(size)])


def gather_four(own, *others):
    beside = swap(own, "tensor", 1)
    across = swap(own, "tensor", 2)
    return [own, beside, across, swap(after(across, *others), "tensor", 1)]


def spread_four(own, near, cross, *others):
    beside = swap(near, "tensor", 1)
    across = swap(cross, "tensor", 2)
    return [own, beside, across, swap(after(across, *others), "tensor", 1)]


def add_low(*parts):
    total = parts[0].astype(F32)
    for part in parts[1:]:
        total = total + part.astype(F32)
    return total.astype(BF16)


def gather_feed_plain(up, down, core):
    pair = jnp.stack([up, down.T])
    pair = lax.all_gather(pair, "tensor", axis=1, tiled=True)
    pair = lax.all_gather(pair, "dp", axis=2, tiled=True)
    pair = pair.reshape(2, pair.shape[1], 8, -1).transpose(0, 2, 1, 3)
    pair = jnp.pad(pair, ((0, 0), (0, 0), (0, 0), (0, BLOCK - pair.shape[3])))
    pair = jnp.where(core == 0, pair, pair[::-1])
    feeds = []
    for half in (pair[0], pair[1]):
        feeds += [half[0], half[1], half[2], half[3], half[4::2], half[5::2]]
    return feeds


def scatter_feed_plain(kept, sent, core, hidden_count):
    grads = jnp.stack([kept, sent]).swapaxes(1, 2).reshape(2, 8, *kept.shape[2:])
    grads = jnp.where(core == 0, grads, grads[::-1]).astype(F32)
    grads = grads[:, :, :, : hidden_count * lax.axis_size("dp") // 8]
    grads = grads.transpose(0, 2, 1, 3).reshape(2, grads.shape[2], -1)
    grads = lax.psum_scatter(grads, "dp", scatter_dimension=2, tiled=True)
    grads = lax.psum_scatter(grads, "tensor", scatter_dimension=1, tiled=True)
    return grads[0], grads[1].T


def sum_pieces(even, odd, norm_sums):
    parts = call(
        add_pieces_kernel,
        (even, swap(odd, "dp", 1)),
        [shape(even.shape[1:], BF16)] * 4,
        limit=4,
    )
    parts = [parts[0]] + [swap(parts[i], "dp", 2 * i) for i in (1, 2, 3)]
    for bit in (2, 1):
        norm_sums = norm_sums + swap(norm_sums, "tensor", bit)
    (own,) = call(
        own_piece_kernel,
        (*parts, norm_sums),
        [shape((even.shape[1] + 16, LANES), BF16)],
        limit=4,
    )
    back = [own] + [swap(own, "dp", e) for e in (2, 4, 6)]
    return back + [swap(jnp.stack(back), "dp", 1)]


def sum_pieces_plain(even, odd, norm_sums):
    even, odd = (lax.psum(part.astype(F32), "dp").astype(BF16) for part in (even, odd))
    norm_sums = lax.psum(norm_sums, ("dp", "tensor"))
    high = norm_sums.astype(BF16)
    rest = (norm_sums - high.astype(F32)).astype(BF16)
    rows = jnp.concatenate([high, rest])
    rows = jnp.pad(rows, ((0, 0), (0, LANES - rows.shape[1])))
    even = jnp.concatenate([even, jnp.stack([rows] + [jnp.zeros_like(rows)] * 3)], axis=1)
    odd = jnp.concatenate([odd, jnp.zeros((4, *rows.shape), BF16)], axis=1)
    return [even[i] for i in range(4)] + [odd]


def shards(
    hidden_in,
    attn_gain,
    attn_shift,
    query_key_value_weight,
    query_key_value_bias,
    attention_output_weight,
    out_bias,
    ffn_gain,
    ffn_shift,
    up_projection_weight,
    up_projection_bias,
    down_projection_weight,
    down_bias,
    lengths,
    cotangent,
):
    chunks = lax.axis_size("tensor")
    ring = lax.axis_size("dp") == 8
    position = lax.axis_index("tensor")
    index = lax.axis_index("dp") if ring else jnp.int32(0)
    core = position & 1
    rows, chunk, width = hidden_in.shape
    full = chunk * chunks
    columns = query_key_value_weight.shape[2]
    heads = columns // HEAD_DIM
    hidden_count = up_projection_weight.shape[1]
    blocks = 8
    half = rows // 2

    info = jnp.stack([position, index]).astype(jnp.int32)
    lengths = lengths.astype(jnp.int32)
    inner_table, outer_table = (jnp.asarray(table) for table in rotary_constants(chunk, chunks))
    hidden = hidden_in.transpose(0, 2, 1)
    given = cotangent.transpose(0, 2, 1)

    if ring:
        inputs = (info, up_projection_weight, down_projection_weight)
        (pair,) = call(
            pair_kernel,
            inputs,
            [shape((columns, 2 * BLOCK), BF16)],
            scratch=[pltpu.VMEM(part.shape, part.dtype) for part in inputs[1:]]
            + [pltpu.SemaphoreType.DMA((2,))],
            in_specs=[smem()] + hbm(2),
            limit=4,
            tiles=20,
        )
        pair_across = swap(pair, "tensor", 2)
    inputs = (
        after(hidden, pair) if ring else hidden,
        attn_gain[None],
        attn_shift[None],
        attention_output_weight,
    )
    first, second = call(
        norm_kernel,
        inputs,
        [
            shape((half * width, chunk), BF16),
            shape((half * width + 2 * columns, chunk), BF16),
        ],
        scratch=[pltpu.VMEM(part.shape, part.dtype) for part in inputs]
        + [pltpu.VMEM((128, width), F32), pltpu.SemaphoreType.DMA((8,))],
        in_specs=hbm(4),
        limit=8,
        tiles=80,
    )
    inputs = (
        info,
        attn_gain[None],
        attn_shift[None],
        out_bias[None],
        ffn_gain[None],
        ffn_shift[None],
        down_bias[None],
        up_projection_bias[None],
        query_key_value_weight,
        query_key_value_bias,
    )
    weight, weight_turned, vectors, bias, up_bias, vector_rows = call(
        lambda *refs: prepare_kernel(heads, *refs),
        inputs,
        [
            shape((3 * columns, width), BF16),
            shape((width, 3 * columns), BF16),
            shape((width, 128), F32),
            shape((3 * columns, 128), F32),
            shape((BLOCK, 128), F32),
            shape((8, width), F32),
        ],
        scratch=[
            pltpu.VMEM((3 * columns, width), F32),
            pltpu.VMEM((128, BLOCK), F32),
        ]
        + [pltpu.VMEM(part.shape, part.dtype) for part in inputs[1:]]
        + [pltpu.SemaphoreType.DMA((9,))],
        in_specs=[smem()] + hbm(len(inputs) - 1),
        limit=8,
        tiles=60,
    )
    if ring:
        parts = [
            pair,
            swap(pair, "tensor", 1),
            pair_across,
            swap(after(pair_across, first), "tensor", 1),
        ]
        (own_feed,) = call(
            lambda *refs: assemble_kernel(chunks, *refs),
            (info, *parts),
            [shape((width, BLOCK), BF16)],
            scratch=[pltpu.VMEM((width, BLOCK), F32)],
            in_specs=[smem()] + vmem(chunks),
            limit=6,
            tiles=20,
        )
        came = [swap(own_feed, "dp", e) for e in (2, 4, 6)]
        beside = swap(own_feed, "dp", 1)
        second_beside = swap(came[0], "dp", 1)
        gathered = [gather_four(first, own_feed)]
    else:
        gathered = [gather_four(first)]

    kept = []
    mixed = []
    for g in range(2):
        if g == 1 and ring:
            gathered[1][0] = after(gathered[1][0], duo, beside, second_beside)
        inputs = (info, lengths, *gathered[g], weight, bias, inner_table, outer_table)
        outs = call(
            lambda *refs, g=g: attend_kernel(heads, chunks, chunk, g * half, half, *refs),
            inputs,
            [
                shape((half, 128, chunk), BF16),
                shape((half, 128, chunk), BF16),
                shape((half, 2, 128, chunk), BF16),
            ]
            + [shape((half, heads, HEAD_ROWS, full), BF16)] * 3
            + [
                shape((half, 8, full), F32),
                shape((half, 128, full), F32),
                shape((half, width, full), BF16),
            ],
            scratch=[
                pltpu.VMEM((heads, full, HEAD_ROWS), BF16),
                pltpu.VMEM((8, full), F32),
                pltpu.VMEM((3 * columns, full), F32),
                pltpu.VMEM((half, width, full), BF16),
                pltpu.SemaphoreType.DMA((half,)),
            ],
            in_specs=[smem(), smem()] + vmem(len(inputs) - 2),
            out_specs=vmem(8) + hbm(),
            limit=14,
            tiles=400,
        )
        kept.append(outs[3:])
        mixed.append(outs[:3])
        if g == 0:
            gathered.append(gather_four(second, outs[0]))
            if ring:
                duo = jnp.stack([after(part, outs[0], second_beside) for part in came[1:]])
                duo_beside = swap(duo, "dp", 1)
            else:
                feeds = gather_feed_plain(up_projection_weight, down_projection_weight, core)

    if ring:
        duo_beside = after(duo_beside, kept[1][0])
        feeds = [own_feed, beside, came[0], second_beside, duo, duo_beside]
        feeds += [swap(part, "tensor", 1) for part in feeds]
    feed_outs = []
    for g in range(2):
        last = g == 1
        others = (kept[1][0],) if g == 0 else (feed_outs[0][2],)
        inputs = (
            info,
            hidden,
            given,
            vectors,
            up_bias,
            *spread_four(*mixed[g], *others),
            *gathered[1],
        )
        if last:
            inputs = inputs + tuple(feed_outs[0][5:]) + (feed_outs[0][0],)
        else:
            inputs = inputs + tuple(feeds)
        carried = [
            shape((2, blocks, width, BLOCK), BF16),
            shape((2, blocks, width, BLOCK), F32),
            shape((chunks, 128, width), F32),
            shape((width, 128), F32),
            shape((BLOCK, 128), F32),
        ]
        sent = [
            shape((2, blocks // 2, width, BLOCK), BF16),
            shape((2, blocks // 2, width, BLOCK), BF16),
            shape((144, LANES), BF16),
            shape((2, 144, LANES), BF16),
            shape((144, LANES), BF16),
        ]
        tokens = half * chunk
        outs = call(
            lambda *refs, g=g, last=last: feed_kernel(
                chunks, blocks, g * half, half, last, *refs
            ),
            inputs,
            [
                shape((rows if last else half, width, chunk), BF16),
                shape((half, width, chunk), F32),
                shape((half, 128, chunk), BF16),
                shape((half, 128, chunk), BF16),
                shape((half, 2, 128, chunk), BF16),
            ]
            + (sent if last else carried),
            scratch=[
                pltpu.VMEM((chunks, 128, width), BF16),
                pltpu.VMEM((chunks, 128, tokens), BF16),
                pltpu.VMEM((width, tokens), F32),
                pltpu.VMEM((width, tokens), BF16),
                pltpu.VMEM((width, tokens), BF16),
                pltpu.VMEM((width, tokens), F32),
                pltpu.VMEM((width, tokens), F32),
                pltpu.VMEM((BLOCK, 128), F32),
                pltpu.SemaphoreType.DMA((2, blocks)),
            ],
            in_specs=[smem()]
            + (
                vmem(len(inputs) - 1)
                if last
                else vmem(len(inputs) - 1 - len(feeds)) + hbm(len(feeds))
            ),
            limit=12,
            tiles=500,
        )
        feed_outs.append(outs)
    hidden_out = feed_outs[1][0]
    middle_grads = [outs[1] for outs in feed_outs]
    feed_kept, feed_sent, out_own, out_near, out_cross = feed_outs[1][5:]

    out_came = swap(out_near, "tensor", 1)
    feed_came = swap(feed_sent, "tensor", 1)
    running = None
    reduced = []
    sums = []
    crossing = []
    mixed_grads = [spread_four(*feed_outs[0][2:5], feed_outs[1][2])]
    for r in range(rows):
        last = r == rows - 1
        g = r // half
        inputs = (
            info,
            lengths,
            *mixed_grads[g],
            *kept[g],
            weight_turned,
            inner_table,
            outer_table,
        )
        if r >= 2:
            running = after(running, sums[r - 2])
        if last:
            running = after(running, reduced[2])
        if last and ring:
            running = after(running, *evens)
        if r > 0:
            inputs = inputs + (running,)
        if last:
            inputs = inputs + (out_own, out_came, out_across, weight, vector_rows)
        outs = call(
            lambda *refs, r=r, last=last: attend_back_kernel(
                heads, chunks, chunk, r, r % half, r == 0, last, *refs
            ),
            inputs,
            [
                shape((width, chunk), BF16),
                shape((2, width, chunk), BF16),
                shape((width, chunk), BF16),
            ]
            + (
                [shape((4, 64, LANES), BF16)] * 2 + [shape((8, width), F32)]
                if last
                else [shape((3 * columns, LANES + 128), F32)]
            ),
            scratch=[
                pltpu.VMEM((128, full), BF16),
                pltpu.VMEM((heads, HEAD_ROWS, full), BF16),
                pltpu.VMEM((heads, HEAD_ROWS, full), BF16),
                pltpu.VMEM((heads, full, HEAD_ROWS), BF16),
                pltpu.VMEM((heads, full, HEAD_ROWS), BF16),
                pltpu.VMEM((3, columns, full), F32),
                pltpu.VMEM((3 * columns, full), BF16),
                pltpu.VMEM((512, LANES), F32),
                pltpu.VMEM((width, full), BF16),
                pltpu.SemaphoreType.DMA(()),
            ],
            in_specs=[smem(), smem()] + vmem(9) + hbm() + vmem(len(inputs) - 12),
            limit=12,
            tiles=420,
        )
        near = swap(outs[1], "tensor", 1)
        reduced += [outs[0], near, None]
        if r < half:
            sums.append(add_low(outs[2], near[1]))
            reduced[-1] = swap(sums[-1], "tensor", 2)
        else:
            crossing.append((outs[2], near))
        if last:
            pair_sum = jnp.stack([add_low(cross, near[1]) for cross, near in crossing])
            reduced[-1] = swap(pair_sum, "tensor", 2)
        if last:
            even, odd, norm_sums = outs[3:]
        else:
            running = outs[3]
        if r == 1:
            mixed_grads.append(spread_four(*feed_outs[1][2:5], outs[0]))
        if r == 0:
            out_across = swap(
                add_low(after(out_cross, outs[0]), out_came[1]), "tensor", 2
            )
            if ring:
                feed_odd = swap(
                    add_low(after(feed_kept[1], outs[0]), feed_came[1]), "dp", 1
                )
        if r == 2 and ring:
            feed_kept = after(feed_kept, outs[0])
            evens = [
                add_low(feed_kept[0, i], feed_came[0, i], feed_odd[i]) for i in range(4)
            ]
            feed_came = [swap(evens[i], "dp", 2 * i) for i in (1, 2, 3)]
    if ring:
        keep, send = call(
            feed_sum_kernel,
            (info, after(evens[0], even), *feed_came),
            [shape((width // 2, BLOCK), BF16)] * 2,
            scratch=[pltpu.VMEM((width, BLOCK), F32)],
            in_specs=[smem()] + vmem(4),
            limit=4,
            tiles=20,
        )
        mine, other = call(
            feed_pair_kernel,
            (info, keep, swap(send, "tensor", 2)),
            [shape((columns, BLOCK), BF16)] * 2,
            scratch=[pltpu.VMEM((width // 2, BLOCK), F32)],
            in_specs=[smem()] + vmem(2),
            limit=4,
            tiles=20,
        )
        feed_parts = (mine, swap(other, "tensor", 1))
    else:
        grad_up_weight, grad_down_weight = scatter_feed_plain(
            feed_kept, feed_sent, core, hidden_count
        )

    parts = (sum_pieces if ring else sum_pieces_plain)(even, odd, norm_sums)
    own_parts = [part for place, part in enumerate(reduced) if place % 3 < 2]
    cross_parts = [part for part in reduced[2::3] if part is not None]
    inputs = (hidden, vectors, *middle_grads, *own_parts, *cross_parts)
    (grad_hidden,) = call(
        lambda *refs: norm_back_kernel(rows, *refs),
        inputs,
        [shape((rows, width, chunk), BF16)],
        limit=12,
        tiles=120,
    )
    parts[0] = after(parts[0], grad_hidden)
    inputs = (info, *parts) + (feed_parts if ring else ())
    outs = [
        shape((3, width, columns), F32),
        shape((3, columns), F32),
        shape((columns, width), F32),
    ]
    outs += [shape((1, width), F32)] * 4
    outs += [shape(up_projection_bias.shape, F32)]
    outs += [shape((1, width), F32)] * 2
    if ring:
        outs += [shape((columns, hidden_count), F32), shape((hidden_count, columns), F32)]
    outs = call(
        unpack_kernel,
        inputs,
        outs,
        scratch=[
            pltpu.VMEM((512, LANES), F32),
            pltpu.VMEM((1, up_projection_bias.shape[0]), F32),
        ],
        in_specs=[smem()] + vmem(len(inputs) - 1),
        limit=8,
        tiles=60,
    )
    grad_qkv_weight, grad_qkv_bias, grad_out_weight = outs[:3]
    grad_ffn_gain, grad_ffn_shift, grad_out_bias, grad_down_bias, grad_up_bias = outs[3:8]
    grad_attn_gain, grad_attn_shift = outs[8:10]
    if ring:
        grad_up_weight, grad_down_weight = outs[10:]
    return (
        hidden_out.transpose(0, 2, 1),
        grad_hidden.transpose(0, 2, 1),
        grad_attn_gain[0],
        grad_attn_shift[0],
        grad_qkv_weight,
        grad_qkv_bias,
        grad_out_weight,
        grad_out_bias[0],
        grad_ffn_gain[0],
        grad_ffn_shift[0],
        grad_up_weight,
        grad_up_bias,
        grad_down_weight,
        grad_down_bias[0],
    )


def solution(mesh):
    return jax.shard_map(
        shards,
        mesh=mesh,
        in_specs=(
            P("dp", "tensor", None),
            P(),
            P(),
            P(None, None, "tensor"),
            P(None, "tensor"),
            P("tensor", None),
            P(),
            P(),
            P(),
            P("tensor", "dp"),
            P(),
            P("dp", "tensor"),
            P(),
            P("dp"),
            P("dp", "tensor", None),
        ),
        out_specs=(
            P("dp", "tensor", None),
            P("dp", "tensor", None),
            P(),
            P(),
            P(None, None, "tensor"),
            P(None, "tensor"),
            P("tensor", None),
            P(),
            P(),
            P(),
            P("tensor", "dp"),
            P(),
            P("dp", "tensor"),
            P(),
        ),
        check_vma=False,
    )
```

time: 852 us -> 266 us (0.31)
  waiting for transfers between devices: 325 us -> 73.8 us
  matrix products: 234 us -> 0 us
  other arithmetic: 134 us -> 1.17 us
  Pallas kernels: 0 us -> 131 us
  blocking collectives: 73.4 us -> 0 us
  local copies, waits for them, and re-layouts: 61.5 us -> 1.63 us
  starting transfers between devices: 1.13 us -> 57.3 us
  between operations: 16.1 us -> 1.46 us
    dot_general x40 -> x0, matrix products: 234 us -> none  [the longest x4 57.4 us: attend_back(): jnp.einsum('hqd,hkd->hqk', grad_one, value_one, preferred_element_type=jn...]
    pallas_call x0 -> x18, Pallas kernels: none -> 131 us  [call(): pl.pallas_call(kernel, out_shape=outs, in_specs=in_specs, out_specs=out_s...]
    reduce_scatter x4 -> x0, waiting for transfers between devices: 124 us -> none  [the longest x1 69.8 us: shards(): lax.psum_scatter(grad_normed_part, 'tensor', scatter_dimension=1, tiled=T...]
    unnamed x13 -> x0, waiting for transfers between devices: 107 us -> none
    convert_element_type x11 -> x5, other arithmetic: 88 us -> 0.82 us  [add_low(): return total.astype(BF16)]
    ppermute x0 -> x59, waiting for transfers between devices: none -> 73.8 us  [swap(): return lax.ppermute(values, axis, [(i, i ^ bit) for i in range(size)])]
    all_gather x4 -> x0, waiting for transfers between devices: 62 us -> none  [the longest x1 34.7 us: shards(): lax.all_gather(first_normalized.astype(jnp.bfloat16), 'tensor', axis=1, t...]
    psum x2 -> x0, blocking collectives: 61.8 us -> none  [the longest x1 39.9 us: shards(): lax.psum((grad_attn_gain, grad_attn_shift, grad_out_bias, grad_ffn_gain,...]
  transfers between devices with their start and end apart: 11 -> 59, of which waited for: 8 -> 17; matrix products, arithmetic and copies ran while one was open for 33% -> 1% of each run, Pallas kernels for 0% -> 40%
where the time goes in v1:
time: 266 us; the launch traced here: 267 us
  Pallas kernels  131 us (49%)
  waiting for transfers between devices  73.8 us (28%)
  starting transfers between devices  57.3 us (22%)
    pallas_call x18, Pallas kernels, call(): pl.pallas_call(kernel, out_shape=outs, in_specs=in_specs, out_specs=out_s...  131 us
    ppermute x59, waiting for transfers between devices, swap(): return lax.ppermute(values, axis, [(i, i ^ bit) for i in range(size)])  73.8 us
    ppermute x59, starting transfers between devices, swap(): return lax.ppermute(values, axis, [(i, i ^ bit) for i in range(size)])  57.3 us
  transfers between devices with their start and end apart: 59, of which 17 were waited for; matrix products, arithmetic and copies ran while one was open for 1% of the time, Pallas kernels for 40%

profile of v1, /device:TPU:0, one launch (start us, length us, event | category | flops | bytes accessed | tf_op | source)
XLA Modules:
  0.0 266.6 jit_solution(7035868546829096136)
XLA Ops:
  2.3 2.0 shard_map.274
  4.3 3.0 %collective-permute-start.5 = (bf16[960,256]{1,0:T(8,128)(2,1)S(1)}, bf16[960,256]{1,0:T(8,128)(2,1)S(1)}, u32[]{:S(2)}, u32[]{:S(2)}) collective-permute-start(bf16[960,256]{1,0:T(8,128)(2,1)S(1)} %get-tuple-element.123.refs_2_), channel_id=1, source_target_pairs={{0,2},{1,3},{2,0},{3,1},{4,6},{5,7},{6,4},{7,5},{8,10},{9,11},{10,... | collective-permute-start | bytes 1474568 | tf_op jit(solution)/shard_map/ppermute | solution.py:787
  7.4 13.8 %collective-permute-done.1.refs_3_ = bf16[120,512]{1,0:T(8,128)(2,1)S(1)} collective-permute-done((bf16[120,512]{1,0:T(8,128)(2,1)S(1)}, bf16[120,512]{1,0:T(8,128)(2,1)S(1)}, u32[]{:S(2)}, u32[]{:S(2)}) %collective-permute-start.1) | collective-permute-done | bytes 122912 | tf_op jit(solution)/shard_map/ppermute | solution.py:787
  23.3 1.8 collective-permute-start.12
  27.3 2.4 shard_map.272
  29.6 3.4 %collective-permute-done.7.refs_15_ = bf16[480,256]{1,0:T(8,128)(2,1)S(1)} collective-permute-done((bf16[480,256]{1,0:T(8,128)(2,1)S(1)}, bf16[480,256]{1,0:T(8,128)(2,1)S(1)}, u32[]{:S(2)}, u32[]{:S(2)}) %collective-permute-start.7) | collective-permute-done | bytes 245792 | tf_op jit(solution)/shard_map/ppermute | solution.py:787
  33.0 3.6 %collective-permute-start.9 = (bf16[480,256]{1,0:T(8,128)(2,1)S(1)}, bf16[480,256]{1,0:T(8,128)(2,1)S(1)}, u32[]{:S(2)}, u32[]{:S(2)}) collective-permute-start(bf16[480,256]{1,0:T(8,128)(2,1)S(1)} %shard_map.275.refs_13_), channel_id=1, source_target_pairs={{0,24},{4,28},{8,16},{12,20},{16,8},{20,12},{24,0},{28,4},{1,25},{... | collective-permute-start | bytes 737288 | tf_op jit(solution)/shard_map/ppermute | solution.py:787
  36.6 1.6 collective-permute-start.8
  38.2 11.6 %shard_map.276 = (bf16[2,128,256]{2,1,0:T(8,128)(2,1)S(1)}, bf16[2,128,256]{2,1,0:T(8,128)(2,1)S(1)}, bf16[2,2,128,256]{3,2,1,0:T(8,128)(2,1)S(1)}, bf16[2,5,32,...) custom-call(s32[2]{0:T(128)S(1)} %pad_add_fusion.refs_0_.info, ...), custom_call_target="tpu_custom_call" | custom-call | flops 1342177280 | tf_op jit(solution)/shard_map/pallas_call | solution.py:58
  50.0 7.0 %collective-permute-done.3 = bf16[480,256]{1,0:T(8,128)(2,1)S(1)} collective-permute-done((bf16[480,256]{1,0:T(8,128)(2,1)S(1)}, bf16[480,256]{1,0:T(8,128)(2,1)S(1)}, u32[]{:S(2)}, u32[]{:S(2)}) %collective-permute-start.3) | collective-permute-done | bytes 245792 | tf_op jit(solution)/shard_map/ppermute | solution.py:787
  57.0 1.6 collective-permute-start.19
  59.1 15.5 %collective-permute-done.10.refs_14_ = bf16[480,256]{1,0:T(8,128)(2,1)S(1)} collective-permute-done((bf16[480,256]{1,0:T(8,128)(2,1)S(1)}, bf16[480,256]{1,0:T(8,128)(2,1)S(1)}, u32[]{:S(2)}, u32[]{:S(2)}) %collective-permute-start.10) | collective-permute-done | bytes 245792 | tf_op jit(solution)/shard_map/ppermute | solution.py:787
  75.6 13.3 %shard_map.277 = (bf16[2,128,256]{2,1,0:T(8,128)(2,1)S(1)}, bf16[2,128,256]{2,1,0:T(8,128)(2,1)S(1)}, bf16[2,2,128,256]{3,2,1,0:T(8,128)(2,1)S(1)}, bf16[2,5,32,...) custom-call(s32[2]{0:T(128)S(1)} %pad_add_fusion.refs_0_.info, ...), custom_call_target="tpu_custom_call" | custom-call | flops 1342177280 | tf_op jit(solution)/shard_map/pallas_call | solution.py:58
  94.1 18.7 %shard_map.278 = (bf16[2,480,256]{2,1,0:T(8,128)(2,1)S(1)}, f32[2,480,256]{2,1,0:T(8,128)S(1)}, bf16[2,128,256]{2,1,0:T(8,128)(2,1)S(1)}, bf16[2,128,256]{2,1,0:...) custom-call(s32[2]{0:T(128)S(1)} %pad_add_fusion.refs_0_.info, ...), custom_call_target="tpu_custom_call" | custom-call | flops 1677721600 | tf_op jit(solution)/shard_map/pallas_call | solution.py:58
  114.6 18.1 %shard_map.279 = (bf16[4,480,256]{2,1,0:T(8,128)(2,1)}, f32[2,480,256]{2,1,0:T(8,128)S(1)}, bf16[2,128,256]{2,1,0:T(8,128)(2,1)S(1)}, bf16[2,128,256]{2,1,0:T(8,...) custom-call(s32[2]{0:T(128)S(1)} %pad_add_fusion.refs_0_.info, ...), custom_call_target="tpu_custom_call" | custom-call | flops 1677721600 | tf_op jit(solution)/shard_map/pallas_call | solution.py:58
  135.4 6.6 %collective-permute-done.28.refs_4_ = bf16[2,2,128,256]{3,2,1,0:T(8,128)(2,1)S(1)} collective-permute-done((bf16[2,2,128,256]{3,2,1,0:T(8,128)(2,1)S(1)}, bf16[2,2,128,256]{3,2,1,0:T(8,128)(2,1)S(1)}, u32[]{:S(2)}, u32[]{:S(2)}) %collective-permute-start.28) | collective-permute-done | bytes 262176 | tf_op jit(solution)/shard_map/ppermute | solution.py:787
  143.6 15.4 %shard_map.280 = (bf16[480,256]{1,0:T(8,128)(2,1)S(1)}, bf16[2,480,256]{2,1,0:T(8,128)(2,1)S(1)}, bf16[480,256]{1,0:T(8,128)(2,1)S(1)}, f32[360,640]{1,0:T(8,128)S(1)}) custom-call(s32[2]{0:T(128)S(1)} %pad_add_fusion.refs_0_.info, s32[4]{0:T(128)S(1)} %copy-done.5, bf16[2,128,256]{2,1,0:T(8,128)(2,1)S(1)} %get-tuple-element.141.refs_2_, ...), custom_call_target="tpu_custom_call" | custom-call | flops 1409286144 | tf_op jit(solution)/shard_map/pallas_call | solution.py:58
  159.5 9.7 %shard_map.281 = (bf16[480,256]{1,0:T(8,128)(2,1)S(1)}, bf16[2,480,256]{2,1,0:T(8,128)(2,1)S(1)}, bf16[480,256]{1,0:T(8,128)(2,1)S(1)}, f32[360,640]{1,0:T(8,128)S(1)}) custom-call(s32[2]{0:T(128)S(1)} %pad_add_fusion.refs_0_.info, s32[4]{0:T(128)S(1)} %copy-done.5, bf16[2,128,256]{2,1,0:T(8,128)(2,1)S(1)} %get-tuple-element.141.refs_2_, ...), custom_call_target="tpu_custom_call" | custom-call | flops 1409286144 | tf_op jit(solution)/shard_map/pallas_call | solution.py:58
  172.1 15.7 %shard_map.282 = (bf16[480,256]{1,0:T(8,128)(2,1)S(1)}, bf16[2,480,256]{2,1,0:T(8,128)(2,1)S(1)}, bf16[480,256]{1,0:T(8,128)(2,1)S(1)}, f32[360,640]{1,0:T(8,128)S(1)}) custom-call(s32[2]{0:T(128)S(1)} %pad_add_fusion.refs_0_.info, s32[4]{0:T(128)S(1)} %copy-done.5, bf16[2,128,256]{2,1,0:T(8,128)(2,1)S(1)} %get-tuple-element.154.refs_2_, ...), custom_call_target="tpu_custom_call" | custom-call | flops 1409286144 | tf_op jit(solution)/shard_map/pallas_call | solution.py:58
  188.4 15.7 %shard_map.283 = (bf16[480,256]{1,0:T(8,128)(2,1)S(1)}, bf16[2,480,256]{2,1,0:T(8,128)(2,1)S(1)}, bf16[480,256]{1,0:T(8,128)(2,1)S(1)}, bf16[4,64,512]{2,1,0:T(8...) custom-call(s32[2]{0:T(128)S(1)} %pad_add_fusion.refs_0_.info, s32[4]{0:T(128)S(1)} %copy-done.5, ...), custom_call_target="tpu_custom_call" | custom-call | flops 1409286144 | tf_op jit(solution)/shard_map/pallas_call | solution.py:58
  205.7 2.7 %collective-permute-done.48 = f32[8,480]{1,0:T(8,128)S(1)} collective-permute-done((f32[8,480]{1,0:T(8,128)S(1)}, f32[8,480]{1,0:T(8,128)S(1)}, u32[]{:S(2)}, u32[]{:S(2)}) %collective-permute-start.48) | collective-permute-done | bytes 15392 | tf_op jit(solution)/shard_map/ppermute | solution.py:787
  208.4 4.4 %collective-permute-done.44.beside = bf16[4,64,512]{2,1,0:T(8,128)(2,1)S(1)} collective-permute-done((bf16[4,64,512]{2,1,0:T(8,128)(2,1)S(1)}, bf16[4,64,512]{2,1,0:T(8,128)(2,1)S(1)}, u32[]{:S(2)}, u32[]{:S(2)}) %collective-permute-start.44) | collective-permute-done | bytes 262176 | tf_op jit(solution)/shard_map/ppermute | solution.py:787
  212.9 4.9 %collective-permute-start.46 = (bf16[64,512]{1,0:T(8,128)(2,1)S(1)}, bf16[64,512]{1,0:T(8,128)(2,1)S(1)}, u32[]{:S(2)}, u32[]{:S(2)}) collective-permute-start(bf16[64,512]{1,0:T(8,128)(2,1)S(1)} %get-tuple-element.203), channel_id=1, source_target_pairs={{0,16},{4,20},{8,24},{12,28},{16,0},{20,4},{24,8},{28,12},{1,17},{... | collective-permute-start | bytes 196616 | tf_op jit(solution)/shard_map/ppermute | solution.py:787
  219.3 2.5 collective-permute-start.56
  221.8 2.9 %collective-permute-done.47.sixth = bf16[64,512]{1,0:T(8,128)(2,1)S(1)} collective-permute-done((bf16[64,512]{1,0:T(8,128)(2,1)S(1)}, bf16[64,512]{1,0:T(8,128)(2,1)S(1)}, u32[]{:S(2)}, u32[]{:S(2)}) %collective-permute-start.47) | collective-permute-done | bytes 65568 | tf_op jit(solution)/shard_map/ppermute | solution.py:787
  224.8 7.4 %collective-permute-start.52 = (bf16[80,512]{1,0:T(8,128)(2,1)S(1)}, bf16[80,512]{1,0:T(8,128)(2,1)S(1)}, u32[]{:S(2)}, u32[]{:S(2)}) collective-permute-start(bf16[80,512]{1,0:T(8,128)(2,1)S(1)} %shard_map.286.refs_0_), channel_id=1, source_target_pairs={{0,24},{4,28},{8,16},{12,20},{16,8},{20,12},{24,0},{28,4},{1,25},{... | collective-permute-start | bytes 245768 | tf_op jit(solution)/shard_map/ppermute | solution.py:787
  235.1 8.0 %collective-permute-start.55 = (bf16[480,256]{1,0:T(8,128)(2,1)S(1)}, bf16[480,256]{1,0:T(8,128)(2,1)S(1)}, u32[]{:S(2)}, u32[]{:S(2)}) collective-permute-start(bf16[480,256]{1,0:T(8,128)(2,1)S(1)} %get-tuple-element.225), channel_id=1, source_target_pairs={{0,16},{4,20},{8,24},{12,28},{16,0},{20,4},{24,8},{28,12},{1,17},{... | collective-permute-start | bytes 737288 | tf_op jit(solution)/shard_map/ppermute | solution.py:787
  243.1 1.7 collective-permute-start.53
  245.9 8.0 %collective-permute-done.55.fourth = bf16[480,256]{1,0:T(8,128)(2,1)S(1)} collective-permute-done((bf16[480,256]{1,0:T(8,128)(2,1)S(1)}, bf16[480,256]{1,0:T(8,128)(2,1)S(1)}, u32[]{:S(2)}, u32[]{:S(2)}) %collective-permute-start.55) | collective-permute-done | bytes 245792 | tf_op jit(solution)/shard_map/ppermute | solution.py:787
  256.7 3.8 %collective-permute-done.57.came = bf16[240,256]{1,0:T(8,128)(2,1)S(1)} collective-permute-done((bf16[240,256]{1,0:T(8,128)(2,1)S(1)}, bf16[240,256]{1,0:T(8,128)(2,1)S(1)}, u32[]{:S(2)}, u32[]{:S(2)}) %collective-permute-start.57) | collective-permute-done | bytes 122912 | tf_op jit(solution)/shard_map/ppermute | solution.py:787
  261.2 3.2 %shard_map.284 = bf16[4,480,256]{2,1,0:T(8,128)(2,1)} custom-call(bf16[4,480,256]{2,1,0:T(8,128)(2,1)S(1)} %bitcast.91, f32[480,128]{1,0:T(8,128)S(1)} %get-tuple-element.119.refs_3_.refs_1_, f32[2,480,256]{2,1,0:T(8,128)S(1)} %get-tuple-element.150.refs_2_, f32[2,480,256]{2,1,0:T(8,128)S(1)} %get-tuple-element.151.refs_3_, ...), custom_call_target="tpu_custom_call" | custom-call | flops 402653184 | tf_op jit(solution)/shard_map/pallas_call | solution.py:58
  264.3 2.0 shard_map.289
  (155 shorter events, 33.5 us)
Async XLA Ops:
  4.3 18.8 %collective-permute-start.5 = (bf16[960,256]{1,0:T(8,128)(2,1)S(1)}, bf16[960,256]{1,0:T(8,128)(2,1)S(1)}, u32[]{:S(2)}, u32[]{:S(2)}) collective-permute-start(bf16[960,256]{1,0:T(8,128)(2,1)S(1)} %get-tuple-element.123.refs_2_), channel_id=1, source_target_pairs={{0,2},{1,3},{2,0},{3,1},{4,6},{5,7},{6,4},{7,5},{8,10},{9,11},{10,... | collective-permute-start | bytes 1474568 | tf_op jit(solution)/shard_map/ppermute | solution.py:787
  7.3 13.9 %collective-permute-start.1 = (bf16[120,512]{1,0:T(8,128)(2,1)S(1)}, bf16[120,512]{1,0:T(8,128)(2,1)S(1)}, u32[]{:S(2)}, u32[]{:S(2)}) collective-permute-start(bf16[120,512]{1,0:T(8,128)(2,1)S(1)} %shard_map.273.refs_1_), channel_id=1, source_target_pairs={{0,2},{1,3},{2,0},{3,1},{4,6},{5,7},{6,4},{7,5},{8,10},{9,11},{10,... | collective-permute-start | bytes 368648 | tf_op jit(solution)/shard_map/ppermute | solution.py:787
  7.4 14.3 %collective-permute-start = (bf16[120,512]{1,0:T(8,128)(2,1)S(1)}, bf16[120,512]{1,0:T(8,128)(2,1)S(1)}, u32[]{:S(2)}, u32[]{:S(2)}) collective-permute-start(bf16[120,512]{1,0:T(8,128)(2,1)S(1)} %shard_map.273.refs_1_), channel_id=1, source_target_pairs={{0,1},{1,0},{2,3},{3,2},{4,5},{5,4},{6,7},{7,6},{8,9},{9,8},{10,11... | collective-permute-start | bytes 368648 | tf_op jit(solution)/shard_map/ppermute | solution.py:787
  21.1 15.5 %collective-permute-start.4 = (bf16[960,256]{1,0:T(8,128)(2,1)S(1)}, bf16[960,256]{1,0:T(8,128)(2,1)S(1)}, u32[]{:S(2)}, u32[]{:S(2)}) collective-permute-start(bf16[960,256]{1,0:T(8,128)(2,1)S(1)} %get-tuple-element.123.refs_2_), channel_id=1, source_target_pairs={{0,1},{1,0},{2,3},{3,2},{4,5},{5,4},{6,7},{7,6},{8,9},{9,8},{10,11... | collective-permute-start | bytes 1474568 | tf_op jit(solution)/shard_map/ppermute | solution.py:787
  23.1 13.5 %collective-permute-start.6 = (bf16[960,256]{1,0:T(8,128)(2,1)S(1)}, bf16[960,256]{1,0:T(8,128)(2,1)S(1)}, u32[]{:S(2)}, u32[]{:S(2)}) collective-permute-start(bf16[960,256]{1,0:T(8,128)(2,1)S(1)} %collective-permute-done.5.refs_4_), channel_id=1, source_target_pairs={{0,1},{1,0},{2,3},{3,2},{4,5},{5,4},{6,7},{7,6},{8,9},{9,8},{10,11... | collective-permute-start | bytes 1474568 | tf_op jit(solution)/shard_map/ppermute | solution.py:787
  23.3 26.5 %collective-permute-start.12 = (bf16[1200,256]{1,0:T(8,128)(2,1)S(1)}, bf16[1200,256]{1,0:T(8,128)(2,1)S(1)}, u32[]{:S(2)}, u32[]{:S(2)}) collective-permute-start(bf16[1200,256]{1,0:T(8,128)(2,1)S(1)} %get-tuple-element.131.refs_2_.refs_9_), channel_id=1, source_target_pairs={{0,2},{1,3},{2,0},{3,1},{4,6},{5,7},{6,4},{7,5},{8,10},{9,11},{10,... | collective-permute-start | bytes 1843208 | tf_op jit(solution)/shard_map/ppermute | solution.py:787
  26.7 47.9 %collective-permute-start.11 = (bf16[1200,256]{1,0:T(8,128)(2,1)S(1)}, bf16[1200,256]{1,0:T(8,128)(2,1)S(1)}, u32[]{:S(2)}, u32[]{:S(2)}) collective-permute-start(bf16[1200,256]{1,0:T(8,128)(2,1)S(1)} %get-tuple-element.131.refs_2_.refs_9_), channel_id=1, source_target_pairs={{0,1},{1,0},{2,3},{3,2},{4,5},{5,4},{6,7},{7,6},{8,9},{9,8},{10,11... | collective-permute-start | bytes 1843208 | tf_op jit(solution)/shard_map/ppermute | solution.py:787
  33.0 16.9 %collective-permute-start.9 = (bf16[480,256]{1,0:T(8,128)(2,1)S(1)}, bf16[480,256]{1,0:T(8,128)(2,1)S(1)}, u32[]{:S(2)}, u32[]{:S(2)}) collective-permute-start(bf16[480,256]{1,0:T(8,128)(2,1)S(1)} %shard_map.275.refs_13_), channel_id=1, source_target_pairs={{0,24},{4,28},{8,16},{12,20},{16,8},{20,12},{24,0},{28,4},{1,25},{... | collective-permute-start | bytes 737288 | tf_op jit(solution)/shard_map/ppermute | solution.py:787
  36.6 20.3 %collective-permute-start.3 = (bf16[480,256]{1,0:T(8,128)(2,1)S(1)}, bf16[480,256]{1,0:T(8,128)(2,1)S(1)}, u32[]{:S(2)}, u32[]{:S(2)}) collective-permute-start(bf16[480,256]{1,0:T(8,128)(2,1)S(1)} %shard_map.275.refs_13_), channel_id=1, source_target_pairs={{0,16},{4,20},{8,24},{12,28},{16,0},{20,4},{24,8},{28,12},{1,17},{... | collective-permute-start | bytes 737288 | tf_op jit(solution)/shard_map/ppermute | solution.py:787
  49.8 25.2 %collective-permute-start.13 = (bf16[1200,256]{1,0:T(8,128)(2,1)S(1)}, bf16[1200,256]{1,0:T(8,128)(2,1)S(1)}, u32[]{:S(2)}, u32[]{:S(2)}) collective-permute-start(bf16[1200,256]{1,0:T(8,128)(2,1)S(1)} %collective-permute-done.12.refs_4_.refs_11_), channel_id=1, source_target_pairs={{0,1},{1,0},{2,3},{3,2},{4,5},{5,4},{6,7},{7,6},{8,9},{9,8},{10,11... | collective-permute-start | bytes 1843208 | tf_op jit(solution)/shard_map/ppermute | solution.py:787
  57.0 32.0 %collective-permute-start.19 = (bf16[2,480,256]{2,1,0:T(8,128)(2,1)S(1)}, bf16[2,480,256]{2,1,0:T(8,128)(2,1)S(1)}, u32[]{:S(2)}, u32[]{:S(2)}) collective-permute-start(bf16[2,480,256]{2,1,0:T(8,128)(2,1)S(1)} %pad_maximum_fusion.refs_17_), channel_id=1, source_target_pairs={{0,4},{4,0},{8,12},{12,8},{16,20},{20,16},{24,28},{28,24},{1,5},{5... | collective-permute-start | bytes 1474568 | tf_op jit(solution)/shard_map/ppermute | solution.py:787
  58.6 16.0 %collective-permute-start.10 = (bf16[480,256]{1,0:T(8,128)(2,1)S(1)}, bf16[480,256]{1,0:T(8,128)(2,1)S(1)}, u32[]{:S(2)}, u32[]{:S(2)}) collective-permute-start(bf16[480,256]{1,0:T(8,128)(2,1)S(1)} %shard_map.275.refs_13_), channel_id=1, source_target_pairs={{0,4},{4,0},{8,12},{12,8},{16,20},{20,16},{24,28},{28,24},{1,5},{5... | collective-permute-start | bytes 737288 | tf_op jit(solution)/shard_map/ppermute | solution.py:787
  59.1 30.0 %collective-permute-start.20 = (bf16[480,256]{1,0:T(8,128)(2,1)S(1)}, bf16[480,256]{1,0:T(8,128)(2,1)S(1)}, u32[]{:S(2)}, u32[]{:S(2)}) collective-permute-start(bf16[480,256]{1,0:T(8,128)(2,1)S(1)} %shard_map.275.refs_13_), channel_id=1, source_target_pairs={{0,1},{1,0},{2,3},{3,2},{4,5},{5,4},{6,7},{7,6},{8,9},{9,8},{10,11... | collective-permute-start | bytes 737288 | tf_op jit(solution)/shard_map/ppermute | solution.py:787
  74.5 15.2 %collective-permute-start.21 = (bf16[480,256]{1,0:T(8,128)(2,1)S(1)}, bf16[480,256]{1,0:T(8,128)(2,1)S(1)}, u32[]{:S(2)}, u32[]{:S(2)}) collective-permute-start(bf16[480,256]{1,0:T(8,128)(2,1)S(1)} %collective-permute-done.10.refs_14_), channel_id=1, source_target_pairs={{0,1},{1,0},{2,3},{3,2},{4,5},{5,4},{6,7},{7,6},{8,9},{9,8},{10,11... | collective-permute-start | bytes 737288 | tf_op jit(solution)/shard_map/ppermute | solution.py:787
  74.5 18.6 %collective-permute-start.24 = (bf16[2,480,256]{2,1,0:T(8,128)(2,1)S(1)}, bf16[2,480,256]{2,1,0:T(8,128)(2,1)S(1)}, u32[]{:S(2)}, u32[]{:S(2)}) collective-permute-start(bf16[2,480,256]{2,1,0:T(8,128)(2,1)S(1)} %pad_maximum_fusion.refs_17_), channel_id=1, source_target_pairs={{0,1},{1,0},{2,3},{3,2},{4,5},{5,4},{6,7},{7,6},{8,9},{9,8},{10,11... | collective-permute-start | bytes 1474568 | tf_op jit(solution)/shard_map/ppermute | solution.py:787
  75.1 14.6 %collective-permute-start.17 = (bf16[2,2,128,256]{3,2,1,0:T(8,128)(2,1)S(1)}, bf16[2,2,128,256]{3,2,1,0:T(8,128)(2,1)S(1)}, u32[]{:S(2)}, u32[]{:S(2)}) collective-permute-start(bf16[2,2,128,256]{3,2,1,0:T(8,128)(2,1)S(1)} %get-tuple-element.137), channel_id=1, source_target_pairs={{0,2},{1,3},{2,0},{3,1},{4,6},{5,7},{6,4},{7,5},{8,10},{9,11},{10,... | collective-permute-start | bytes 786440 | tf_op jit(solution)/shard_map/ppermute | solution.py:787
  91.6 21.2 %collective-permute-start.15 = (bf16[2,2,128,256]{3,2,1,0:T(8,128)(2,1)S(1)}, bf16[2,2,128,256]{3,2,1,0:T(8,128)(2,1)S(1)}, u32[]{:S(2)}, u32[]{:S(2)}) collective-permute-start(bf16[2,2,128,256]{3,2,1,0:T(8,128)(2,1)S(1)} %get-tuple-element.135), channel_id=1, source_target_pairs={{0,2},{1,3},{2,0},{3,1},{4,6},{5,7},{6,4},{7,5},{8,10},{9,11},{10,... | collective-permute-start | bytes 786440 | tf_op jit(solution)/shard_map/ppermute | solution.py:787
  132.7 26.5 %collective-permute-start.37 = (bf16[2,4,480,256]{3,2,1,0:T(8,128)(2,1)S(1)}, bf16[2,4,480,256]{3,2,1,0:T(8,128)(2,1)S(1)}, u32[]{:S(2)}, u32[]{:S(2)}) collective-permute-start(bf16[2,4,480,256]{3,2,1,0:T(8,128)(2,1)S(1)} %get-tuple-element.187), channel_id=1, source_target_pairs={{0,1},{1,0},{2,3},{3,2},{4,5},{5,4},{6,7},{7,6},{8,9},{9,8},{10,11... | collective-permute-start | bytes 5898248 | tf_op jit(solution)/shard_map/ppermute | solution.py:787
  134.0 37.1 %collective-permute-start.32 = (bf16[2,128,256]{2,1,0:T(8,128)(2,1)S(1)}, bf16[2,128,256]{2,1,0:T(8,128)(2,1)S(1)}, u32[]{:S(2)}, u32[]{:S(2)}) collective-permute-start(bf16[2,128,256]{2,1,0:T(8,128)(2,1)S(1)} %get-tuple-element.168), channel_id=1, source_target_pairs={{0,1},{1,0},{2,3},{3,2},{4,5},{5,4},{6,7},{7,6},{8,9},{9,8},{10,11... | collective-permute-start | bytes 393224 | tf_op jit(solution)/shard_map/ppermute | solution.py:787
  134.4 34.8 %collective-permute-start.33 = (bf16[2,2,128,256]{3,2,1,0:T(8,128)(2,1)S(1)}, bf16[2,2,128,256]{3,2,1,0:T(8,128)(2,1)S(1)}, u32[]{:S(2)}, u32[]{:S(2)}) collective-permute-start(bf16[2,2,128,256]{3,2,1,0:T(8,128)(2,1)S(1)} %get-tuple-element.169), channel_id=1, source_target_pairs={{0,2},{1,3},{2,0},{3,1},{4,6},{5,7},{6,4},{7,5},{8,10},{9,11},{10,... | collective-permute-start | bytes 786440 | tf_op jit(solution)/shard_map/ppermute | solution.py:787
  142.1 27.6 %collective-permute-start.39 = (bf16[2,144,512]{2,1,0:T(8,128)(2,1)S(1)}, bf16[2,144,512]{2,1,0:T(8,128)(2,1)S(1)}, u32[]{:S(2)}, u32[]{:S(2)}) collective-permute-start(bf16[2,144,512]{2,1,0:T(8,128)(2,1)S(1)} %get-tuple-element.191), channel_id=1, source_target_pairs={{0,1},{1,0},{2,3},{3,2},{4,5},{5,4},{6,7},{7,6},{8,9},{9,8},{10,11... | collective-permute-start | bytes 884744 | tf_op jit(solution)/shard_map/ppermute | solution.py:787
  159.4 28.5 %collective-permute-start.38 = (bf16[4,480,256]{2,1,0:T(8,128)(2,1)S(1)}, bf16[4,480,256]{2,1,0:T(8,128)(2,1)S(1)}, u32[]{:S(2)}, u32[]{:S(2)}) collective-permute-start(bf16[4,480,256]{2,1,0:T(8,128)(2,1)S(1)} %fusion), channel_id=1, source_target_pairs={{0,4},{4,0},{8,12},{12,8},{16,20},{20,16},{24,28},{28,24},{1,5},{5... | collective-permute-start | bytes 2949128 | tf_op jit(solution)/shard_map/ppermute | solution.py:787
  169.7 18.1 %collective-permute-start.31 = (bf16[2,480,256]{2,1,0:T(8,128)(2,1)S(1)}, bf16[2,480,256]{2,1,0:T(8,128)(2,1)S(1)}, u32[]{:S(2)}, u32[]{:S(2)}) collective-permute-start(bf16[2,480,256]{2,1,0:T(8,128)(2,1)S(1)} %get-tuple-element.167), channel_id=1, source_target_pairs={{0,1},{1,0},{2,3},{3,2},{4,5},{5,4},{6,7},{7,6},{8,9},{9,8},{10,11... | collective-permute-start | bytes 1474568 | tf_op jit(solution)/shard_map/ppermute | solution.py:787
  169.9 18.5 %collective-permute-start.40 = (bf16[144,512]{1,0:T(8,128)(2,1)S(1)}, bf16[144,512]{1,0:T(8,128)(2,1)S(1)}, u32[]{:S(2)}, u32[]{:S(2)}) collective-permute-start(bf16[144,512]{1,0:T(8,128)(2,1)S(1)} %fusion.9), channel_id=1, source_target_pairs={{0,2},{1,3},{2,0},{3,1},{4,6},{5,7},{6,4},{7,5},{8,10},{9,11},{10,... | collective-permute-start | bytes 442376 | tf_op jit(solution)/shard_map/ppermute | solution.py:787
  171.1 16.9 %collective-permute-start.36 = (bf16[480,256]{1,0:T(8,128)(2,1)S(1)}, bf16[480,256]{1,0:T(8,128)(2,1)S(1)}, u32[]{:S(2)}, u32[]{:S(2)}) collective-permute-start(bf16[480,256]{1,0:T(8,128)(2,1)S(1)} %fusion.8), channel_id=1, source_target_pairs={{0,2},{1,3},{2,0},{3,1},{4,6},{5,7},{6,4},{7,5},{8,10},{9,11},{10,... | collective-permute-start | bytes 737288 | tf_op jit(solution)/shard_map/ppermute | solution.py:787
  187.9 30.0 %collective-permute-start.35 = (bf16[2,480,256]{2,1,0:T(8,128)(2,1)S(1)}, bf16[2,480,256]{2,1,0:T(8,128)(2,1)S(1)}, u32[]{:S(2)}, u32[]{:S(2)}) collective-permute-start(bf16[2,480,256]{2,1,0:T(8,128)(2,1)S(1)} %get-tuple-element.180), channel_id=1, source_target_pairs={{0,1},{1,0},{2,3},{3,2},{4,5},{5,4},{6,7},{7,6},{8,9},{9,8},{10,11... | collective-permute-start | bytes 1474568 | tf_op jit(solution)/shard_map/ppermute | solution.py:787
  204.1 29.1 %collective-permute-start.41 = (bf16[2,480,256]{2,1,0:T(8,128)(2,1)S(1)}, bf16[2,480,256]{2,1,0:T(8,128)(2,1)S(1)}, u32[]{:S(2)}, u32[]{:S(2)}) collective-permute-start(bf16[2,480,256]{2,1,0:T(8,128)(2,1)S(1)} %get-tuple-element.196), channel_id=1, source_target_pairs={{0,1},{1,0},{2,3},{3,2},{4,5},{5,4},{6,7},{7,6},{8,9},{9,8},{10,11... | collective-permute-start | bytes 1474568 | tf_op jit(solution)/shard_map/ppermute | solution.py:787
  219.3 25.5 %collective-permute-start.56 = (bf16[480,256]{1,0:T(8,128)(2,1)S(1)}, bf16[480,256]{1,0:T(8,128)(2,1)S(1)}, u32[]{:S(2)}, u32[]{:S(2)}) collective-permute-start(bf16[480,256]{1,0:T(8,128)(2,1)S(1)} %get-tuple-element.224), channel_id=1, source_target_pairs={{0,24},{4,28},{8,16},{12,20},{16,8},{20,12},{24,0},{28,4},{1,25},{... | collective-permute-start | bytes 737288 | tf_op jit(solution)/shard_map/ppermute | solution.py:787
  233.4 27.8 %collective-permute-start.43 = (bf16[2,480,256]{2,1,0:T(8,128)(2,1)S(1)}, bf16[2,480,256]{2,1,0:T(8,128)(2,1)S(1)}, u32[]{:S(2)}, u32[]{:S(2)}) collective-permute-start(bf16[2,480,256]{2,1,0:T(8,128)(2,1)S(1)} %pad_maximum_fusion.1), channel_id=1, source_target_pairs={{0,2},{1,3},{2,0},{3,1},{4,6},{5,7},{6,4},{7,5},{8,10},{9,11},{10,... | collective-permute-start | bytes 1474568 | tf_op jit(solution)/shard_map/ppermute | solution.py:787
  235.1 18.8 %collective-permute-start.55 = (bf16[480,256]{1,0:T(8,128)(2,1)S(1)}, bf16[480,256]{1,0:T(8,128)(2,1)S(1)}, u32[]{:S(2)}, u32[]{:S(2)}) collective-permute-start(bf16[480,256]{1,0:T(8,128)(2,1)S(1)} %get-tuple-element.225), channel_id=1, source_target_pairs={{0,16},{4,20},{8,24},{12,28},{16,0},{20,4},{24,8},{28,12},{1,17},{... | collective-permute-start | bytes 737288 | tf_op jit(solution)/shard_map/ppermute | solution.py:787
  243.1 21.2 %collective-permute-start.53 = (bf16[4,80,512]{2,1,0:T(8,128)(2,1)S(1)}, bf16[4,80,512]{2,1,0:T(8,128)(2,1)S(1)}, u32[]{:S(2)}, u32[]{:S(2)}) collective-permute-start(bf16[4,80,512]{2,1,0:T(8,128)(2,1)S(1)} %pad_maximum_fusion.2), channel_id=1, source_target_pairs={{0,4},{4,0},{8,12},{12,8},{16,20},{20,16},{24,28},{28,24},{1,5},{5... | collective-permute-start | bytes 983048 | tf_op jit(solution)/shard_map/ppermute | solution.py:787
  244.8 16.3 %collective-permute-start.42 = (bf16[480,256]{1,0:T(8,128)(2,1)S(1)}, bf16[480,256]{1,0:T(8,128)(2,1)S(1)}, u32[]{:S(2)}, u32[]{:S(2)}) collective-permute-start(bf16[480,256]{1,0:T(8,128)(2,1)S(1)} %fusion.7), channel_id=1, source_target_pairs={{0,2},{1,3},{2,0},{3,1},{4,6},{5,7},{6,4},{7,5},{8,10},{9,11},{10,... | collective-permute-start | bytes 737288 | tf_op jit(solution)/shard_map/ppermute | solution.py:787
  (45 other events, 543.5 us)
